TPU v7x, 256 devices: a whole 4x4x8 slice. The times are simulated.
256 devices in a mesh: grp: 8 (over z), cur: 32 (over y, x, core).
Axes of the slice: x: 4, y: 4, z: 8, core: 2. Of those that a mesh axis runs over, the one named last changes fastest.
Arguments:
- right_side: float32 [3, 2097152], P(None, ('grp', 'cur')), may hold values from -6 to 6
- precond: float32 [2097152], P(('grp', 'cur')), may hold values from 0.3 to 3
- viscosity: float32 [262144], P(('grp', 'cur')), may hold values from 0.1 to 10
- stiffness: float32 [81, 81], replicated
- element_nodes: int32 [27, 262144], P(None, ('grp', 'cur')), may hold values from 0 to 9471
- live_elements: int32 [256], P(('grp', 'cur')), may hold values from 256 to 1024, as said below
- shared_nodes: int32 [2, 131072], P(None, ('grp', 'cur')), may hold values from 0 to 8191, as said below
- hanging_parents: int32 [3, 65536], P(None, ('grp', 'cur')), may hold values from 0 to 9215
Outputs:
- solution: float32 [3, 2097152], P(None, ('grp', 'cur'))
- residual: float32 [3, 2097152], P(None, ('grp', 'cur'))
Inputs may be any that keep to these rules, and one draw needn't show every extreme that they name: `element_nodes`: local numbers: below 8192 owned, then 512 copies from the previous device, 512 from the next, then the hanging nodes. `hanging_parents`: parents are owned nodes or copies. `shared_nodes`: within one device, the 1024 entries are distinct owned nodes (no node in both rows). `live_elements`: some device has all 1024 slots live.
All inputs are finite; a program needn't handle non-finite values.
Results may differ from a plain program's by a relative error of at most 0.0004.
Values sent between devices are 32-bit elements; how exact they have to be, the bound alone decides.
A program may use at most 128 MiB of HBM per device.

v0:
```python
import jax
import jax.numpy as jnp
from jax import lax
from jax.sharding import PartitionSpec as P

ITERS = 3


def padded(block, sides, width):
    for axis, dim in sides:
        count = lax.axis_size(axis)
        forward = [(i, i + 1) for i in range(count - 1)]
        backward = [(target, source) for source, target in forward]
        low = lax.ppermute(
            lax.slice_in_dim(block, block.shape[dim] - width, None, axis=dim), axis, forward
        )
        high = lax.ppermute(lax.slice_in_dim(block, 0, width, axis=dim), axis, backward)
        block = jnp.concatenate([low, block, high], axis=dim)
    return block


def add_hanging(base, parents):
    hanging = 0.375 * base[:, parents[0]] + 0.75 * base[:, parents[1]] - 0.125 * base[:, parents[2]]
    return jnp.concatenate([base, hanging], 1)


def fold_hanging(partial_value, width, parents):
    hanging_part = partial_value[:, width:]
    base_part = partial_value[:, :width]
    base_part = base_part.at[:, parents[0]].add(0.375 * hanging_part)
    base_part = base_part.at[:, parents[1]].add(0.75 * hanging_part)
    return base_part.at[:, parents[2]].add(-0.125 * hanging_part)


def element_terms(extended, cells, weighting, transposed):
    width = cells.shape[1]
    values_in = extended[:, cells.reshape(-1)].reshape(81, width)
    values_out = (
        jnp.dot(transposed, values_in, precision=lax.Precision.HIGHEST) * weighting[None, :]
    )
    return values_out.reshape(3, 27 * width)


def residual_norm(residual, search):
    return lax.psum(jnp.sum(residual * search), ("grp", "cur"))


def local(
    right_side,
    precond,
    viscosity,
    stiffness,
    element_nodes,
    live_elements,
    shared_nodes,
    hanging_parents,
):
    owned = right_side.shape[1]
    ghost_count = shared_nodes.shape[1]
    elements = element_nodes.shape[1]
    send_left = shared_nodes[0]
    send_right = shared_nodes[1]
    live_count = live_elements[0]
    live_mask = (jnp.arange(elements, dtype=jnp.int32) < live_count).astype(jnp.float32)
    weighting = viscosity * live_mask
    transposed = stiffness.T
    residual = right_side
    solution = jnp.zeros((3, owned), jnp.float32)
    search = precond * residual
    norm_now = residual_norm(residual, search)
    for iteration in range(ITERS):
        outgoing_values = jnp.concatenate([search[:, send_left], search[:, send_right]], 1)
        arrived = padded(outgoing_values, ((("grp", "cur"), 1),), ghost_count)
        operator_base = jnp.concatenate(
            [search, arrived[:, :ghost_count], arrived[:, 3 * ghost_count :]], 1
        )
        extended = add_hanging(operator_base, hanging_parents)
        empty = jnp.zeros((3, extended.shape[1]), jnp.float32)
        partial_value = empty.at[:, element_nodes.reshape(-1)].add(
            element_terms(extended, element_nodes, weighting, transposed)
        )
        operator_partial_value = fold_hanging(
            partial_value, operator_base.shape[1], hanging_parents
        )
        returned = padded(operator_partial_value[:, owned:], ((("grp", "cur"), 1),), ghost_count)
        image = (
            operator_partial_value[:, :owned]
            .at[:, send_left]
            .add(returned[:, :ghost_count])
            .at[:, send_right]
            .add(returned[:, 3 * ghost_count :])
        )
        own_search = search
        curvature = lax.psum(jnp.sum(own_search * image), ("grp", "cur"))
        step_size = norm_now / curvature
        solution = solution + step_size * own_search
        residual = residual - step_size * image
        search = precond * residual
        if iteration + 1 < ITERS:
            norm_now = residual_norm(residual, search)
    return (solution, residual)


def solution(mesh):
    in_specs = (
        P(None, ("grp", "cur")),
        P(("grp", "cur")),
        P(("grp", "cur")),
        P(),
        P(None, ("grp", "cur")),
        P(("grp", "cur")),
        P(None, ("grp", "cur")),
        P(None, ("grp", "cur")),
    )
    out_specs = (P(None, ("grp", "cur")), P(None, ("grp", "cur")))
    return jax.shard_map(local, mesh=mesh, in_specs=in_specs, out_specs=out_specs, check_vma=False)
```

profile of v0, /device:TPU:1, one launch (start us, length us, event | category | flops | bytes accessed | tf_op | source)
XLA Modules:
  0.0 1252.8 jit_solution(793720114386255488)
XLA Ops:
  8.4 4.5 collective-permute-start
  36.5 93.7 %gather_fusion.5 = f32[27648,3]{1,0:T(8,128)} fusion(f32[3,9472]{0,1:T(8,128)} %copy.118, s32[27648]{0:T(1024)S(1)} %broadcast_clamp_fusion), kind=kCustom, calls=%fused_computation.5 | custom fusion | bytes 774144 | tf_op jit(solution)/shard_map/gather | solution.py:37
  130.3 8.3 copy.119
  139.5 7.7 copy.120
  147.2 136.3 %scatter_custom_fusion = f32[3,9472]{0,1:T(8,128)} fusion(s32[27648]{0:T(1024)S(1)} %bitcast.107, f32[3,27648]{0,1:T(8,128)} %copy.120, f32[]{:T(128)} %constant.9.clone.1), kind=kCustom, calls=%fused_computation.40 | custom fusion | flops 82944 | bytes 445444 | tf_op jit(solution)/shard_map/scatter-add | solution.py:79
  287.4 6.6 scatter_custom_fusion.1
  294.0 6.6 scatter_custom_fusion.2
  300.6 6.6 scatter_custom_fusion.3
  312.8 4.5 slice.142
  317.2 7.2 scatter_custom_fusion.4
  324.5 7.2 scatter_custom_fusion.5
  335.2 85.1 %all-reduce.2 = (f32[]{:T(128)}, f32[]{:T(128)}) all-reduce(f32[]{:T(128)} %get-tuple-element.15, f32[]{:T(128)} %get-tuple-element.14), channel_id=1, replica_groups=mesh['grp'=8,'cur'=32] {'grp','cur'}, use_global_device_ids=true, to_apply=%region_1.0 | all-reduce | flops 2 | bytes 16 | tf_op jit(solution)/shard_map/psum | solution.py:45
  454.0 93.7 %gather_fusion.11 = f32[27648,3]{1,0:T(8,128)} fusion(f32[3,9472]{0,1:T(8,128)} %copy.133, s32[27648]{0:T(1024)S(1)} %broadcast_clamp_fusion), kind=kCustom, calls=%fused_computation.11 | custom fusion | bytes 774144 | tf_op jit(solution)/shard_map/gather | solution.py:37
  547.8 8.3 copy.134
  557.0 7.7 copy.135
  564.7 136.5 %scatter_custom_fusion.6 = f32[3,9472]{0,1:T(8,128)} fusion(s32[27648]{0:T(1024)S(1)} %bitcast.108, f32[3,27648]{0,1:T(8,128)} %copy.135, f32[]{:T(128)} %constant.9.clone.1), kind=kCustom, calls=%fused_computation.38 | custom fusion | flops 82944 | bytes 445444 | tf_op jit(solution)/shard_map/scatter-add | solution.py:79
  705.1 6.6 scatter_custom_fusion.7
  711.7 6.6 scatter_custom_fusion.8
  718.3 6.6 scatter_custom_fusion.9
  734.8 7.2 scatter_custom_fusion.10
  742.0 7.2 scatter_custom_fusion.11
  752.7 82.5 %all-reduce.1 = (f32[]{:T(128)}, f32[]{:T(128)}) all-reduce(f32[]{:T(128)} %get-tuple-element.13, f32[]{:T(128)} %get-tuple-element.12), channel_id=1, replica_groups=mesh['grp'=8,'cur'=32] {'grp','cur'}, use_global_device_ids=true, to_apply=%region_11.0 | all-reduce | flops 2 | bytes 16 | tf_op jit(solution)/shard_map/psum | solution.py:45
  868.9 93.7 %gather_fusion.17 = f32[27648,3]{1,0:T(8,128)} fusion(f32[3,9472]{0,1:T(8,128)} %copy.148, s32[27648]{0:T(1024)S(1)} %broadcast_clamp_fusion), kind=kCustom, calls=%fused_computation.17 | custom fusion | bytes 774144 | tf_op jit(solution)/shard_map/gather | solution.py:37
  962.6 8.3 copy.149
  971.9 7.7 copy.150
  979.6 136.3 %scatter_custom_fusion.12 = f32[3,9472]{0,1:T(8,128)} fusion(s32[27648]{0:T(1024)S(1)} %bitcast.109, f32[3,27648]{0,1:T(8,128)} %copy.150, f32[]{:T(128)} %constant.9.clone.1), kind=kCustom, calls=%fused_computation.36 | custom fusion | flops 82944 | bytes 445444 | tf_op jit(solution)/shard_map/scatter-add | solution.py:79
  1119.8 6.6 scatter_custom_fusion.13
  1126.4 6.6 scatter_custom_fusion.14
  1132.9 6.6 scatter_custom_fusion.15
  1149.4 7.5 scatter_custom_fusion.16
  1156.9 7.2 scatter_custom_fusion.17
  1167.7 82.5 %all-reduce = (f32[]{:T(128)}, f32[]{:T(128)}) all-reduce(f32[]{:T(128)} %get-tuple-element.11, f32[]{:T(128)} %get-tuple-element.10), channel_id=1, replica_groups=mesh['grp'=8,'cur'=32] {'grp','cur'}, use_global_device_ids=true, to_apply=%region_21.0 | all-reduce | flops 2 | bytes 16 | tf_op jit(solution)/shard_map/psum | solution.py:45
  (121 shorter events, 146.6 us)
Async XLA Ops:
  0.6 138.1 %copy-start = (f32[81,81]{1,0:T(8,128)S(1)}, f32[81,81]{1,0:T(8,128)}, u32[]{:S(2)}) copy-start(f32[81,81]{1,0:T(8,128)} %param.11) | copy-start | bytes 78736
  0.6 18.2 %copy-start.5 = (s32[3,256]{1,0:T(4,128)S(1)}, s32[3,256]{1,0:T(4,128)}, u32[]{:S(2)}) copy-start(s32[3,256]{1,0:T(4,128)} %param.15) | copy-start | bytes 9220
  0.7 18.2 %copy-start.3 = (s32[27,1024]{1,0:T(8,128)S(1)}, s32[27,1024]{1,0:T(8,128)}, u32[]{:S(2)}) copy-start(s32[27,1024]{1,0:T(8,128)} %param.12) | copy-start | bytes 331780
  0.7 18.5 %copy-start.4 = (f32[1024]{0:T(1024)S(1)}, f32[1024]{0:T(1024)}, u32[]{:S(2)}) copy-start(f32[1024]{0:T(1024)} %param.10) | copy-start | bytes 12292
  8.4 10.8 collective-permute-start
  16.2 5.0 collective-permute-start.1
  308.2 9.0 collective-permute-start.2
  310.2 14.3 %collective-permute-start.3 = (f32[3,512]{0,1:T(8,128)S(1)}, f32[3,512]{0,1:T(8,128)S(1)}, u32[]{:S(2)}, u32[]{:S(2)}) collective-permute-start(f32[3,512]{0,1:T(8,128)S(1)} %get-tuple-element.30), channel_id=1, source_target_pairs={{1,0},{2,1},{3,2},{4,3},{5,4},{6,5},{7,6},{8,7},{9,8},{10,9},{11,1... | collective-permute-start | bytes 18440 | tf_op jit(solution)/shard_map/ppermute | solution.py:17
  324.4 10.1 copy-start.1
  324.4 10.1 copy-start.2
  431.0 4.6 collective-permute-start.4
  433.7 5.0 collective-permute-start.5
  725.9 8.8 collective-permute-start.6
  727.9 14.1 %collective-permute-start.7 = (f32[3,512]{0,1:T(8,128)S(1)}, f32[3,512]{0,1:T(8,128)S(1)}, u32[]{:S(2)}, u32[]{:S(2)}) collective-permute-start(f32[3,512]{0,1:T(8,128)S(1)} %get-tuple-element.28), channel_id=1, source_target_pairs={{1,0},{2,1},{3,2},{4,3},{5,4},{6,5},{7,6},{8,7},{9,8},{10,9},{11,1... | collective-permute-start | bytes 18440 | tf_op jit(solution)/shard_map/ppermute | solution.py:17
  845.9 4.9 collective-permute-start.8
  848.6 5.0 collective-permute-start.9
  1140.6 8.8 collective-permute-start.10
  1142.6 14.4 %collective-permute-start.11 = (f32[3,512]{0,1:T(8,128)S(1)}, f32[3,512]{0,1:T(8,128)S(1)}, u32[]{:S(2)}, u32[]{:S(2)}) collective-permute-start(f32[3,512]{0,1:T(8,128)S(1)} %get-tuple-element.26), channel_id=1, source_target_pairs={{1,0},{2,1},{3,2},{4,3},{5,4},{6,5},{7,6},{8,7},{9,8},{10,9},{11,1... | collective-permute-start | bytes 18440 | tf_op jit(solution)/shard_map/ppermute | solution.py:17
where the time goes:
time: 1260 us; the launch traced here: 1250 us
  other arithmetic  517 us (41%)
  local copies, waits for them, and re-layouts  441 us (35%)
  blocking collectives  250 us (20%)
  starting transfers between devices  29.1 us (2%)
    scatter-add x3, other arithmetic, local(): empty.at[:, element_nodes.reshape(-1)]  409 us
    gather x6, local copies, waits for them, and re-layouts, element_terms(): values_in = extended[:, cells.reshape(-1)].reshape(81, width)  306 us
    psum x3, blocking collectives, residual_norm(): return lax.psum(jnp.sum(residual * search), ('grp', 'cur'))  250 us
    scatter-add x6, other arithmetic, local(): image = operator_partial_value[:, :owned].at[:, send_left].add(returned[:...  43.5 us
  transfers between devices with their start and end apart: 12, of which 3 were waited for; matrix products, arithmetic and copies ran while one was open for 3% of the time, Pallas kernels for 0%

commit v1 on v0

v1 whole, which is shorter than its diff:
```python
import functools

import jax
import jax.numpy as jnp
from jax import lax
from jax.experimental import pallas as pl
from jax.experimental.pallas import tpu as pltpu
from jax.sharding import PartitionSpec as P

ITERS = 3
F32 = jnp.float32
BF16 = jnp.bfloat16
MESH = pl.DeviceIdType.MESH
OWN_ROWS = 64
EXT_ROWS = 74
STEP_K = 3


def take(src, lanes):
    return jnp.take_along_axis(src, lanes, axis=1, mode="promise_in_bounds")


def gather_tile(fields, row_count, index):
    lanes = index & 127
    rows = index >> 7
    found = [jnp.zeros((8, 128), F32) for _ in fields]
    for row in range(row_count):
        hit = rows == row
        for i, field in enumerate(fields):
            line = jnp.broadcast_to(field(row), (8, 128))
            found[i] = jnp.where(hit, take(line, lanes), found[i])
    return found


def folded(index):
    row = index >> 7
    lane = index & 127
    own = row < 64
    hang = row >= 72
    band = jnp.where(own, row & 31, jnp.where(hang, 36, 32 + (row & 3)))
    half = jnp.where(own, row >> 5, jnp.where(hang, row & 1, (row >> 2) & 1))
    return band, half * 128 + lane


def pieces(row):
    high = row.astype(BF16)
    low = (row - high.astype(F32)).astype(BF16)
    return high, low


def spread_dot(band, place, values, extra=True):
    n = band.shape[1]
    band16 = band.astype(jnp.int16)
    place16 = place.astype(jnp.int16)
    zero = jnp.zeros((16, n), BF16)
    one = jnp.ones((256, n), BF16)
    hot = jnp.where(
        lax.broadcasted_iota(jnp.int16, (256, n), 0) == place16, one, jnp.zeros((256, n), BF16)
    )
    line = lax.broadcasted_iota(jnp.int16, (16, n), 0)
    hit0 = line == band16
    hit1 = (line + jnp.int16(16)) == band16
    parts = []
    tails = []
    if extra:
        first = line < jnp.int16(8)
        hit2 = jnp.where(first, line, line - jnp.int16(8)) == (band16 - jnp.int16(32))
    for value in values:
        high, low = pieces(value)
        high = jnp.broadcast_to(high, (16, n))
        low = jnp.broadcast_to(low, (16, n))
        for piece in (high, low):
            parts.append(jnp.where(hit0, piece, zero))
            parts.append(jnp.where(hit1, piece, zero))
        if extra:
            tails.append(jnp.where(hit2, jnp.where(first, high, low), zero))
    left = jnp.concatenate(parts + tails, 0)
    return lax.dot_general(left, hot, (((1,), (1,)), ((), ())), preferred_element_type=F32)


def own_part(total, c):
    return total[c * 64 : c * 64 + 32] + total[c * 64 + 32 : c * 64 + 64]


def extra_part(total, c):
    return total[192 + c * 16 : 200 + c * 16] + total[200 + c * 16 : 208 + c * 16]


def kernel(
    rounds,
    sizes,
    rhs_ref,
    pre_ref,
    visc_ref,
    stiff_ref,
    cells_ref,
    live_ref,
    shared_ref,
    parents_ref,
    sol_ref,
    res_ref,
    ext_ref,
    gres_ref,
    gpre_ref,
    band_ref,
    place_ref,
    u_ref,
    t_ref,
    acc_ref,
    part_ref,
    send_ref,
    recv_ref,
    red_ref,
    sum_ref,
    send_sem,
    recv_sem,
    rsend_sem,
    rrecv_sem,
):
    n_grp, n_cur = sizes
    devices = n_grp * n_cur
    my_grp = lax.axis_index("grp")
    my_cur = lax.axis_index("cur")
    me = my_grp * n_cur + my_cur

    def ring(offset):
        other = lax.rem(me + offset + devices, devices)
        return {"grp": other // n_cur, "cur": lax.rem(other, n_cur)}

    def partner(r, j):
        axis, stride, size = rounds[r]
        mine = my_cur if axis == "cur" else my_grp
        place = lax.rem(mine // stride, size)
        return {axis: mine + (lax.rem(place + j, size) - place) * stride}

    def my_place(r):
        axis, stride, size = rounds[r]
        mine = my_cur if axis == "cur" else my_grp
        return lax.rem(mine // stride, size)

    barrier = pltpu.get_barrier_semaphore()
    targets = [ring(-1), ring(1)]
    for r, (_, _, size) in enumerate(rounds):
        targets += [partner(r, j) for j in range(1, size)]
    for target in targets:
        pl.semaphore_signal(barrier, inc=1, device_id=target, device_id_type=MESH)

    band, place = folded(cells_ref[...])
    band_ref[0:27, :] = band
    place_ref[0:27, :] = place
    shared_index = jnp.concatenate(
        [shared_ref[j : j + 1, q * 128 : (q + 1) * 128] for j in range(2) for q in range(4)], 0
    )
    parent_rows = [parents_ref[p : p + 1, q * 128 : (q + 1) * 128] for p in range(3) for q in range(2)]
    parent_index = jnp.concatenate(parent_rows + parent_rows[:2], 0)
    shared_band, shared_place = folded(
        jnp.concatenate([shared_ref[0:1, :], shared_ref[1:2, :]], 1)
    )
    parent_band, parent_place = folded(
        jnp.concatenate([parents_ref[p : p + 1, :] for p in range(3)], 1)
    )
    slot = lax.broadcasted_iota(jnp.int32, (1, 1024), 1)
    weight = jnp.where(slot < live_ref[0], visc_ref[...], 0.0)
    at = lax.broadcasted_iota(jnp.int32, (96, 81), 0)
    want = jnp.where((at & 31) < 27, (at >> 5) * 27 + (at & 31), -1)
    pick = jnp.where(want == lax.broadcasted_iota(jnp.int32, (96, 81), 1), 1.0, 0.0).astype(BF16)

    def padded(part):
        rows = lax.dot_general(pick, part, (((1,), (1,)), ((), ())), preferred_element_type=F32)
        return lax.dot_general(
            rows.astype(BF16), pick, (((1,), (1,)), ((), ())), preferred_element_type=F32
        ).astype(BF16)

    stiff = stiff_ref[...]
    stiff_high = stiff.astype(BF16)
    stiff_low = padded((stiff - stiff_high.astype(F32)).astype(BF16))
    stiff_high = padded(stiff_high)

    u_ref[...] = jnp.zeros_like(u_ref)
    for c in range(3):
        res_ref[c] = rhs_ref[c]
        sol_ref[c] = jnp.zeros((OWN_ROWS, 128), F32)
        ext_ref[c, 0:OWN_ROWS, :] = pre_ref[...] * rhs_ref[c]

    def exchange(number):
        copies = []
        for side, offset in ((0, -1), (1, 1)):
            copies.append(
                pltpu.make_async_remote_copy(
                    src_ref=send_ref.at[number, side],
                    dst_ref=recv_ref.at[number, 1 - side],
                    send_sem=send_sem.at[number, side],
                    recv_sem=recv_sem.at[number, 1 - side],
                    device_id=ring(offset),
                    device_id_type=MESH,
                )
            )
        for copy in copies:
            copy.start()
        return copies

    outgoing = gather_tile(
        [lambda row, c=c: rhs_ref[c, row : row + 1, :] for c in range(3)]
        + [lambda row: pre_ref[row : row + 1, :]],
        OWN_ROWS,
        shared_index,
    )
    for side in range(2):
        for c in range(3):
            send_ref[0, side, c, 0:4, :] = outgoing[c][side * 4 : side * 4 + 4]
            send_ref[0, side, c, 4:8, :] = outgoing[3][side * 4 : side * 4 + 4]
    pl.semaphore_wait(barrier, len(targets))
    copies = exchange(0)
    for copy in copies:
        copy.wait()
    has = [
        jnp.where(me > 0, 1.0, 0.0).astype(F32),
        jnp.where(me < devices - 1, 1.0, 0.0).astype(F32),
    ]
    for side in range(2):
        for c in range(3):
            gres_ref[c, side * 4 : side * 4 + 4, :] = recv_ref[0, side, c, 0:4, :]
        gpre_ref[side * 4 : side * 4 + 4, :] = recv_ref[0, side, 0, 4:8, :] * has[side]
    for c in range(3):
        ext_ref[c, OWN_ROWS : OWN_ROWS + 8, :] = gpre_ref[...] * gres_ref[c]

    def reduce_send(it, r):
        _, _, size = rounds[r]
        spot = my_place(r)
        sends = []
        for j in range(1, size):
            sends.append(
                pltpu.make_async_remote_copy(
                    src_ref=sum_ref.at[it, r],
                    dst_ref=red_ref.at[it, r, spot],
                    send_sem=rsend_sem.at[it, r],
                    recv_sem=rrecv_sem.at[it, r],
                    device_id=partner(r, j),
                    device_id_type=MESH,
                )
            )
        red_ref[it, r, spot] = sum_ref[it, r]
        for send in sends:
            send.start()

    def reduce_wait(it, r):
        _, _, size = rounds[r]
        block = red_ref.at[it, r, pl.ds(0, size - 1)]
        pltpu.make_async_copy(block, block, rrecv_sem.at[it, r]).wait()
        total = red_ref[it, r, 0]
        for j in range(1, size):
            total = total + red_ref[it, r, j]
        return total

    for it in range(ITERS):
        found = gather_tile(
            [lambda row, c=c: ext_ref[c, row : row + 1, :] for c in range(3)], 72, parent_index
        )
        for c in range(3):
            ext_ref[c, 72:74, :] = (
                0.375 * found[c][0:2] + 0.75 * found[c][2:4] - 0.125 * found[c][4:6]
            )
        fields = [lambda row, c=c: ext_ref[c, row : row + 1, :] for c in range(3)]

        def gather_rows(tile, _):
            top = pl.multiple_of(tile * 8, 8)
            for j in range(8):
                columns = slice(j * 128, j * 128 + 128)
                got = gather_tile(fields, EXT_ROWS, cells_ref[pl.ds(top, 8), columns])
                for c in range(3):
                    u_ref[c, pl.ds(top, 8), columns] = got[c]
            return 0

        lax.fori_loop(0, 3, gather_rows, 0)
        for k in range(24, 27):
            index = jnp.concatenate(
                [cells_ref[k : k + 1, s * 128 : s * 128 + 128] for s in range(8)], 0
            )
            got = gather_tile(fields, EXT_ROWS, index)
            for c in range(3):
                for s in range(8):
                    u_ref[c, k : k + 1, s * 128 : s * 128 + 128] = got[c][s : s + 1]

        u = u_ref[...].reshape(96, 1024)
        u_high = u.astype(BF16)
        u_low = (u - u_high.astype(F32)).astype(BF16)
        t = (
            jnp.dot(stiff_high, u_high, preferred_element_type=F32)
            + jnp.dot(stiff_high, u_low, preferred_element_type=F32)
            + jnp.dot(stiff_low, u_high, preferred_element_type=F32)
        ) * weight
        t_ref[...] = t
        bent = jnp.sum(u * t, 0, keepdims=True)
        bent = sum(bent[:, j * 128 : j * 128 + 128] for j in range(8))
        norm = sum(res_ref[c] * ext_ref[c, 0:OWN_ROWS, :] for c in range(3))
        norm = jnp.sum(norm, 0, keepdims=True)
        sum_ref[it, 0] = jnp.concatenate(
            [jnp.broadcast_to(norm, (4, 128)), jnp.broadcast_to(bent, (4, 128))], 0
        )
        reduce_send(it, 0)

        acc_ref[...] = jnp.zeros_like(acc_ref)

        def scatter_step(step, _):
            bands, places, values = [], [], [[], [], []]
            for i in range(STEP_K):
                k = step * STEP_K + i
                bands.append(band_ref[pl.ds(k, 1), :])
                places.append(place_ref[pl.ds(k, 1), :])
                for c in range(3):
                    values[c].append(t_ref[pl.ds(c * 32 + k, 1), :])
            acc_ref[...] += spread_dot(
                jnp.concatenate(bands, 1),
                jnp.concatenate(places, 1),
                [jnp.concatenate(v, 1) for v in values],
            )
            return 0

        steps = 27 // STEP_K
        marks = [steps * i // len(rounds) for i in range(len(rounds) + 1)]
        for r in range(len(rounds)):
            if r > 0:
                sum_ref[it, r] = reduce_wait(it, r - 1)
                reduce_send(it, r)
            lax.fori_loop(marks[r], marks[r + 1], scatter_step, 0)

        hanging = [extra_part(acc_ref, c)[4:5] for c in range(3)]
        fold = spread_dot(
            parent_band,
            parent_place,
            [jnp.concatenate([0.375 * h, 0.75 * h, -0.125 * h], 1) for h in hanging],
        )
        copied = []
        for c in range(3):
            own = own_part(acc_ref, c) + own_part(fold, c)
            part_ref[c, 0:32, :] = own[:, 0:128]
            part_ref[c, 32:64, :] = own[:, 128:256]
            copied.append((extra_part(acc_ref, c) + extra_part(fold, c))[0:4])
        outgoing = gather_tile(
            [lambda row, c=c: part_ref[c, row : row + 1, :] for c in range(3)],
            OWN_ROWS,
            shared_index,
        )
        number = it + 1
        for side in range(2):
            for c in range(3):
                send_ref[number, side, c, 0:4, :] = outgoing[c][side * 4 : side * 4 + 4]
                send_ref[number, side, c, 4:8, :] = copied[c][:, side * 128 : side * 128 + 128]
        copies = exchange(number)
        total = reduce_wait(it, len(rounds) - 1)
        norm = jnp.sum(total[0:1], 1, keepdims=True)
        bent = jnp.sum(total[4:5], 1, keepdims=True)
        step = norm / bent
        for copy in copies:
            copy.wait()
        back = []
        for c in range(3):
            rows = [
                recv_ref[number, side, c, 4 + q : 5 + q, :] * has[side]
                for side in range(2)
                for q in range(4)
            ]
            back.append(jnp.concatenate(rows, 1))
        returned = spread_dot(shared_band, shared_place, back, extra=False)
        for c in range(3):
            add = own_part(returned, c)
            search = ext_ref[c, 0:OWN_ROWS, :]
            image = part_ref[c] + jnp.concatenate([add[:, 0:128], add[:, 128:256]], 0)
            sol_ref[c] = sol_ref[c] + step * search
            residual = res_ref[c] - step * image
            res_ref[c] = residual
            if it + 1 < ITERS:
                ext_ref[c, 0:OWN_ROWS, :] = pre_ref[...] * residual
                for side in range(2):
                    own = slice(side * 4, side * 4 + 4)
                    image = recv_ref[number, side, c, 0:4, :] + send_ref[number, side, c, 4:8, :]
                    gres_ref[c, own, :] = gres_ref[c, own, :] - step * image
                ext_ref[c, OWN_ROWS : OWN_ROWS + 8, :] = gpre_ref[...] * gres_ref[c]

    for it in range(ITERS):
        for r, (_, _, size) in enumerate(rounds):
            block = red_ref.at[it, r, pl.ds(0, size - 1)]
            pltpu.make_async_copy(block, block, rsend_sem.at[it, r]).wait()


def make_local(n_grp, n_cur):
    rounds = []
    rest, stride = n_cur, 1
    while rest > 1:
        size = min(8, rest)
        rounds.append(("cur", stride, size))
        stride, rest = stride * size, rest // size
    if n_grp > 1:
        rounds.append(("grp", 1, n_grp))
    widest = max(size for _, _, size in rounds)

    def local(
        right_side, precond, viscosity, stiffness, element_nodes, live, shared, parents
    ):
        vmem = pl.BlockSpec(memory_space=pltpu.VMEM)
        smem = pl.BlockSpec(memory_space=pltpu.SMEM)
        shape = jax.ShapeDtypeStruct((3, OWN_ROWS, 128), F32)
        call = pl.pallas_call(
            functools.partial(kernel, tuple(rounds), (n_grp, n_cur)),
            out_shape=(shape, shape),
            in_specs=[vmem, vmem, vmem, vmem, vmem, smem, vmem, vmem],
            out_specs=(vmem, vmem),
            scratch_shapes=[
                pltpu.VMEM((3, 80, 128), F32),
                pltpu.VMEM((3, 8, 128), F32),
                pltpu.VMEM((8, 128), F32),
                pltpu.VMEM((32, 1024), jnp.int32),
                pltpu.VMEM((32, 1024), jnp.int32),
                pltpu.VMEM((3, 32, 1024), F32),
                pltpu.VMEM((96, 1024), F32),
                pltpu.VMEM((240, 256), F32),
                pltpu.VMEM((3, OWN_ROWS, 128), F32),
                pltpu.VMEM((ITERS + 1, 2, 3, 8, 128), F32),
                pltpu.VMEM((ITERS + 1, 2, 3, 8, 128), F32),
                pltpu.VMEM((ITERS, len(rounds), widest, 8, 128), F32),
                pltpu.VMEM((ITERS, len(rounds), 8, 128), F32),
                pltpu.SemaphoreType.DMA((ITERS + 1, 2)),
                pltpu.SemaphoreType.DMA((ITERS + 1, 2)),
                pltpu.SemaphoreType.DMA((ITERS, len(rounds))),
                pltpu.SemaphoreType.DMA((ITERS, len(rounds))),
            ],
            compiler_params=pltpu.CompilerParams(
                collective_id=0, has_side_effects=True, vmem_limit_bytes=48 * 1024 * 1024
            ),
            name="descent",
        )
        sol, res = call(
            right_side.reshape(3, OWN_ROWS, 128),
            precond.reshape(OWN_ROWS, 128),
            viscosity.reshape(1, 1024),
            stiffness,
            element_nodes,
            live,
            shared,
            parents,
        )
        return sol.reshape(3, OWN_ROWS * 128), res.reshape(3, OWN_ROWS * 128)

    return local


def solution(mesh):
    both = ("grp", "cur")
    in_specs = (
        P(None, both),
        P(both),
        P(both),
        P(),
        P(None, both),
        P(both),
        P(None, both),
        P(None, both),
    )
    out_specs = (P(None, both), P(None, both))
    return jax.shard_map(
        make_local(mesh.shape["grp"], mesh.shape["cur"]),
        mesh=mesh,
        in_specs=in_specs,
        out_specs=out_specs,
        check_vma=False,
    )
```

time: 1260 us -> 78 us (0.06)
  other arithmetic: 517 us -> 0 us
  local copies, waits for them, and re-layouts: 441 us -> 1.81 us
  blocking collectives: 250 us -> 0 us
  Pallas kernels: 0 us -> 74.7 us
  starting transfers between devices: 29.1 us -> 0 us
    scatter-add x18 -> x0, other arithmetic: 512 us -> none  [the longest x3 409 us: local(): empty.at[:, element_nodes.reshape(-1)]]
    gather x36 -> x0, local copies, waits for them, and re-layouts: 354 us -> none  [the longest x6 306 us: element_terms(): values_in = extended[:, cells.reshape(-1)].reshape(81, width)]
    psum x3 -> x0, blocking collectives: 250 us -> none  [residual_norm(): return lax.psum(jnp.sum(residual * search), ('grp', 'cur'))]
    pallas_call x0 -> x1, Pallas kernels: none -> 74.7 us  [local(): call(right_side.reshape(3, OWN_ROWS, 128), precond.reshape(OWN_ROWS, 128)...]
    ppermute x12 -> x0, starting transfers between devices: 29.1 us -> none  [the longest x6 15.7 us: padded(): lax.ppermute(lax.slice_in_dim(block, block.shape[dim] - width, None, axis...]
    slice x9 -> x0, local copies, waits for them, and re-layouts: 28.4 us -> none  [the longest x3 13.4 us: local(): operator_partial_value[:, :owned].at[:, send_left]]
    reshape x9 -> x1, local copies, waits for them, and re-layouts: 24.4 us -> 0.83 us  [local(): return (sol.reshape(3, OWN_ROWS * 128), res.reshape(3, OWN_ROWS * 128))]
    concatenate x6 -> x0, local copies, waits for them, and re-layouts: 17.5 us -> none  [the longest x3 8.85 us: add_hanging(): return jnp.concatenate([base, hanging], 1)]
  transfers between devices with their start and end apart: 12 -> 0, of which waited for: 3 -> 0; matrix products, arithmetic and copies ran while one was open for 3% -> 0% of each run, Pallas kernels for 0% -> 0%
where the time goes in v1:
time: 78 us; the launch traced here: 77.9 us
  Pallas kernels  74.7 us (96%)
  local copies, waits for them, and re-layouts  1.81 us (2%)
  between operations  1.41 us (2%)
    pallas_call x1, Pallas kernels, local(): call(right_side.reshape(3, OWN_ROWS, 128), precond.reshape(OWN_ROWS, 128)...  74.7 us

profile of v1, /device:TPU:1, one launch (start us, length us, event | category | flops | bytes accessed | tf_op | source)
XLA Modules:
  0.0 77.9 jit_solution(2694808933270580090)
XLA Ops:
  0.6 0.0 copy-start
  1.3 0.0 copy-start.1
  1.3 0.0 copy-start.2
  1.3 0.0 copy-start.3
  1.4 0.0 copy-start.4
  1.4 0.0 copy-start.5
  1.4 0.9 %copy.16 = f32[1,3,64,128]{3,2,1,0:T(8,128)S(1)} copy(f32[1,3,64,128]{3,1,2,0:T(4,128)} %bitcast.17) | data formatting | bytes 196608
  2.3 0.0 copy-done
  2.3 0.0 copy-done.1
  2.3 0.0 copy-done.2
  2.3 0.0 copy-done.3
  2.4 0.0 copy-done.4
  2.4 0.0 copy-done.5
  2.4 74.7 %descent.1 = (f32[3,64,128]{2,1,0:T(8,128)S(1)}, f32[3,64,128]{2,1,0:T(8,128)S(1)}) custom-call(f32[3,64,128]{2,1,0:T(8,128)S(1)} %bitcast.12, f32[64,128]{1,0:T(8,128)S(1)} %bitcast.15, f32[1,1024]{1,0:T(1,128)S(1)} %bitcast.16, f32[81,81]{1,0:T(8,128)S(1)} %copy-done.1, s32[27,1024]{1,0:T(8,128)S(1)} %copy-done, s32[1]{0:T(128)S(6)} %copy.17.live_ref, ...), custom_call_target="tpu_custom_call" | custom-call | tf_op jit(solution)/shard_map/descent/pallas_call | solution.py:432
  77.1 0.8 %copy_bitcast_fusion = (f32[3,8192]{1,0:T(4,128)}, f32[3,8192]{1,0:T(4,128)}) fusion(f32[1,3,64,128]{3,2,1,0:T(8,128)S(1)} %bitcast.14, f32[1,3,64,128]{3,2,1,0:T(8,128)S(1)} %bitcast.13), kind=kLoop, calls=%fused_computation | loop fusion | bytes 393216 | tf_op jit(solution)/shard_map/reshape | solution.py:442
Async XLA Ops:
  0.6 1.7 %copy-start = (s32[27,1024]{1,0:T(8,128)S(1)}, s32[27,1024]{1,0:T(8,128)}, u32[]{:S(2)}) copy-start(s32[27,1024]{1,0:T(8,128)} %cells_ref.1) | copy-start | bytes 331780
  1.3 1.0 %copy-start.1 = (f32[81,81]{1,0:T(8,128)S(1)}, f32[81,81]{1,0:T(8,128)}, u32[]{:S(2)}) copy-start(f32[81,81]{1,0:T(8,128)} %stiff_ref.1) | copy-start | bytes 78736
  1.3 1.0 %copy-start.2 = (f32[8192]{0:T(1024)S(1)}, f32[8192]{0:T(1024)}, u32[]{:S(2)}) copy-start(f32[8192]{0:T(1024)} %param.9) | copy-start | bytes 98308
  1.3 1.0 %copy-start.3 = (f32[1024]{0:T(1024)S(1)}, f32[1024]{0:T(1024)}, u32[]{:S(2)}) copy-start(f32[1024]{0:T(1024)} %param.10) | copy-start | bytes 12292
  1.4 1.0 %copy-start.4 = (s32[2,512]{1,0:T(2,128)S(1)}, s32[2,512]{1,0:T(2,128)}, u32[]{:S(2)}) copy-start(s32[2,512]{1,0:T(2,128)} %shared_ref.1) | copy-start | bytes 12292
  1.4 1.0 %copy-start.5 = (s32[3,256]{1,0:T(4,128)S(1)}, s32[3,256]{1,0:T(4,128)}, u32[]{:S(2)}) copy-start(s32[3,256]{1,0:T(4,128)} %parents_ref.1) | copy-start | bytes 9220

commit v2 on v1

--- a/solution.py
+++ b/solution.py
@@ -13,7 +13,8 @@
 MESH = pl.DeviceIdType.MESH
 OWN_ROWS = 64
 EXT_ROWS = 74
-STEP_K = 3
+CHUNKS = 8
+NODES = 28
 
 
 def take(src, lanes):
@@ -86,6 +87,38 @@
     return total[192 + c * 16 : 200 + c * 16] + total[200 + c * 16 : 208 + c * 16]
 
 
+def chunk_dot(band_ref, place_ref, piece_ref, columns):
+    zero = jnp.zeros((16, 128), BF16)
+    one = jnp.ones((16, 128), BF16)
+    line = lax.broadcasted_iota(jnp.int16, (16, 128), 0)
+    lines = [line + jnp.int16(16 * i) for i in range(16)]
+    first = line < jnp.int16(8)
+    beyond = jnp.where(first, line, line - jnp.int16(8)) + jnp.int16(32)
+    hots, lefts = [], []
+    for k in range(NODES):
+        band = jnp.broadcast_to(band_ref[k : k + 1, columns], (16, 128)).astype(jnp.int16)
+        place = jnp.broadcast_to(place_ref[k : k + 1, columns], (16, 128)).astype(jnp.int16)
+        hots.append(jnp.concatenate([jnp.where(at == place, one, zero) for at in lines], 0))
+        hits = [lines[0] == band, lines[1] == band]
+        hit_beyond = beyond == band
+        parts, tails = [], []
+        for c in range(3):
+            row = c * 32 + k
+            pair = [
+                jnp.broadcast_to(piece_ref[p, row : row + 1, :], (16, 128)).astype(BF16)
+                for p in range(2)
+            ]
+            parts += [jnp.where(hit, piece, zero) for piece in pair for hit in hits]
+            tails.append(jnp.where(hit_beyond, jnp.where(first, pair[0], pair[1]), zero))
+        lefts.append(jnp.concatenate(parts + tails, 0))
+    return lax.dot_general(
+        jnp.concatenate(lefts, 1),
+        jnp.concatenate(hots, 1),
+        (((1,), (1,)), ((), ())),
+        preferred_element_type=F32,
+    )
+
+
 def kernel(
     rounds,
     sizes,
@@ -100,14 +133,19 @@
     sol_ref,
     res_ref,
     ext_ref,
-    gres_ref,
+    search_ref,
+    image_ref,
+    gimage_ref,
     gpre_ref,
+    weight_ref,
+    matrix_ref,
     band_ref,
     place_ref,
     u_ref,
-    t_ref,
+    piece_ref,
     acc_ref,
     part_ref,
+    step_ref,
     send_ref,
     recv_ref,
     red_ref,
@@ -127,16 +165,16 @@
         other = lax.rem(me + offset + devices, devices)
         return {"grp": other // n_cur, "cur": lax.rem(other, n_cur)}
 
-    def partner(r, j):
-        axis, stride, size = rounds[r]
-        mine = my_cur if axis == "cur" else my_grp
-        place = lax.rem(mine // stride, size)
-        return {axis: mine + (lax.rem(place + j, size) - place) * stride}
-
     def my_place(r):
         axis, stride, size = rounds[r]
         mine = my_cur if axis == "cur" else my_grp
         return lax.rem(mine // stride, size)
+
+    def partner(r, j):
+        axis, stride, size = rounds[r]
+        mine = my_cur if axis == "cur" else my_grp
+        place = my_place(r)
+        return {axis: mine + (lax.rem(place + j, size) - place) * stride}
 
     barrier = pltpu.get_barrier_semaphore()
     targets = [ring(-1), ring(1)]
@@ -145,6 +183,8 @@
     for target in targets:
         pl.semaphore_signal(barrier, inc=1, device_id=target, device_id_type=MESH)
 
+    band_ref[24:32, :] = jnp.zeros((8, 1024), jnp.int32)
+    place_ref[24:32, :] = jnp.zeros((8, 1024), jnp.int32)
     band, place = folded(cells_ref[...])
     band_ref[0:27, :] = band
     place_ref[0:27, :] = place
@@ -160,7 +200,7 @@
         jnp.concatenate([parents_ref[p : p + 1, :] for p in range(3)], 1)
     )
     slot = lax.broadcasted_iota(jnp.int32, (1, 1024), 1)
-    weight = jnp.where(slot < live_ref[0], visc_ref[...], 0.0)
+    weight_ref[...] = jnp.where(slot < live_ref[0], visc_ref[...], 0.0)
     at = lax.broadcasted_iota(jnp.int32, (96, 81), 0)
     want = jnp.where((at & 31) < 27, (at >> 5) * 27 + (at & 31), -1)
     pick = jnp.where(want == lax.broadcasted_iota(jnp.int32, (96, 81), 1), 1.0, 0.0).astype(BF16)
@@ -173,14 +213,20 @@
 
     stiff = stiff_ref[...]
     stiff_high = stiff.astype(BF16)
-    stiff_low = padded((stiff - stiff_high.astype(F32)).astype(BF16))
-    stiff_high = padded(stiff_high)
+    matrix_ref[0] = padded(stiff_high)
+    matrix_ref[1] = padded((stiff - stiff_high.astype(F32)).astype(BF16))
 
     u_ref[...] = jnp.zeros_like(u_ref)
+    gimage_ref[...] = jnp.zeros_like(gimage_ref)
+    step_ref[0] = jnp.zeros((8, 128), F32)
+    step_ref[1] = jnp.full((8, 128), -1.0, F32)
     for c in range(3):
         res_ref[c] = rhs_ref[c]
         sol_ref[c] = jnp.zeros((OWN_ROWS, 128), F32)
-        ext_ref[c, 0:OWN_ROWS, :] = pre_ref[...] * rhs_ref[c]
+        image_ref[c] = jnp.zeros((OWN_ROWS, 128), F32)
+        search = pre_ref[...] * rhs_ref[c]
+        ext_ref[c, 0:OWN_ROWS, :] = search
+        search_ref[c] = search
 
     def exchange(number):
         copies = []
@@ -218,30 +264,26 @@
         jnp.where(me < devices - 1, 1.0, 0.0).astype(F32),
     ]
     for side in range(2):
-        for c in range(3):
-            gres_ref[c, side * 4 : side * 4 + 4, :] = recv_ref[0, side, c, 0:4, :]
-        gpre_ref[side * 4 : side * 4 + 4, :] = recv_ref[0, side, 0, 4:8, :] * has[side]
-    for c in range(3):
-        ext_ref[c, OWN_ROWS : OWN_ROWS + 8, :] = gpre_ref[...] * gres_ref[c]
+        own = slice(side * 4, side * 4 + 4)
+        gpre_ref[own, :] = recv_ref[0, side, 0, 4:8, :] * has[side]
+        for c in range(3):
+            ext_ref[c, OWN_ROWS + side * 4 : OWN_ROWS + side * 4 + 4, :] = (
+                gpre_ref[own, :] * recv_ref[0, side, c, 0:4, :]
+            )
 
     def reduce_send(it, r):
         _, _, size = rounds[r]
         spot = my_place(r)
-        sends = []
+        red_ref[it, r, spot] = sum_ref[it, r]
         for j in range(1, size):
-            sends.append(
-                pltpu.make_async_remote_copy(
-                    src_ref=sum_ref.at[it, r],
-                    dst_ref=red_ref.at[it, r, spot],
-                    send_sem=rsend_sem.at[it, r],
-                    recv_sem=rrecv_sem.at[it, r],
-                    device_id=partner(r, j),
-                    device_id_type=MESH,
-                )
-            )
-        red_ref[it, r, spot] = sum_ref[it, r]
-        for send in sends:
-            send.start()
+            pltpu.make_async_remote_copy(
+                src_ref=sum_ref.at[it, r],
+                dst_ref=red_ref.at[it, r, spot],
+                send_sem=rsend_sem.at[it, r],
+                recv_sem=rrecv_sem.at[it, r],
+                device_id=partner(r, j),
+                device_id_type=MESH,
+            ).start()
 
     def reduce_wait(it, r):
         _, _, size = rounds[r]
@@ -252,77 +294,81 @@
             total = total + red_ref[it, r, j]
         return total
 
-    for it in range(ITERS):
-        found = gather_tile(
-            [lambda row, c=c: ext_ref[c, row : row + 1, :] for c in range(3)], 72, parent_index
-        )
+    def reduce_step(it, r):
+        sum_ref[it, r] = reduce_wait(it, r - 1)
+        reduce_send(it, r)
+
+    def reduce_end(it):
+        total = reduce_wait(it, len(rounds) - 1)
+        norm = jnp.sum(total[0:1], 1, keepdims=True)
+        bent = jnp.sum(total[4:5], 1, keepdims=True)
+        step = jnp.broadcast_to(norm / bent, (8, 128))
+        step_ref[0] = step
+        step_ref[1] = step
+
+    fields = [lambda row, c=c: ext_ref[c, row : row + 1, :] for c in range(3)]
+    marks = [1 + (6 * r) // len(rounds) for r in range(len(rounds))]
+
+    def columns_of(chunk):
+        if isinstance(chunk, int):
+            return pl.ds(chunk * 128, 128)
+        return pl.ds(pl.multiple_of(chunk * 128, 128), 128)
+
+    def gather(chunk):
+        for top in range(0, 24, 8):
+            got = gather_tile(fields, EXT_ROWS, cells_ref[top : top + 8, columns_of(chunk)])
+            for c in range(3):
+                u_ref[chunk, c, top : top + 8, :] = got[c]
+
+    def element(chunk):
+        u = u_ref[chunk].reshape(96, 128)
+        u_high = u.astype(BF16)
+        u_low = (u - u_high.astype(F32)).astype(BF16)
+        high, low = matrix_ref[0], matrix_ref[1]
+        t = (
+            jnp.dot(high, u_high, preferred_element_type=F32)
+            + jnp.dot(high, u_low, preferred_element_type=F32)
+            + jnp.dot(low, u_high, preferred_element_type=F32)
+        ) * weight_ref[0:1, columns_of(chunk)]
+        t_high = t.astype(BF16).astype(F32)
+        piece_ref[0] = t_high
+        piece_ref[1] = t - t_high
+
+    def scatter(chunk):
+        acc_ref[...] += chunk_dot(band_ref, place_ref, piece_ref, columns_of(chunk))
+
+    def iteration(it, _):
+        found = gather_tile(fields, 72, parent_index)
         for c in range(3):
             ext_ref[c, 72:74, :] = (
                 0.375 * found[c][0:2] + 0.75 * found[c][2:4] - 0.125 * found[c][4:6]
             )
-        fields = [lambda row, c=c: ext_ref[c, row : row + 1, :] for c in range(3)]
-
-        def gather_rows(tile, _):
-            top = pl.multiple_of(tile * 8, 8)
-            for j in range(8):
-                columns = slice(j * 128, j * 128 + 128)
-                got = gather_tile(fields, EXT_ROWS, cells_ref[pl.ds(top, 8), columns])
-                for c in range(3):
-                    u_ref[c, pl.ds(top, 8), columns] = got[c]
-            return 0
-
-        lax.fori_loop(0, 3, gather_rows, 0)
+        acc_ref[...] = jnp.zeros_like(acc_ref)
         for k in range(24, 27):
             index = jnp.concatenate(
-                [cells_ref[k : k + 1, s * 128 : s * 128 + 128] for s in range(8)], 0
+                [cells_ref[k : k + 1, s * 128 : s * 128 + 128] for s in range(CHUNKS)], 0
             )
             got = gather_tile(fields, EXT_ROWS, index)
             for c in range(3):
-                for s in range(8):
-                    u_ref[c, k : k + 1, s * 128 : s * 128 + 128] = got[c][s : s + 1]
-
-        u = u_ref[...].reshape(96, 1024)
-        u_high = u.astype(BF16)
-        u_low = (u - u_high.astype(F32)).astype(BF16)
-        t = (
-            jnp.dot(stiff_high, u_high, preferred_element_type=F32)
-            + jnp.dot(stiff_high, u_low, preferred_element_type=F32)
-            + jnp.dot(stiff_low, u_high, preferred_element_type=F32)
-        ) * weight
-        t_ref[...] = t
-        bent = jnp.sum(u * t, 0, keepdims=True)
-        bent = sum(bent[:, j * 128 : j * 128 + 128] for j in range(8))
-        norm = sum(res_ref[c] * ext_ref[c, 0:OWN_ROWS, :] for c in range(3))
-        norm = jnp.sum(norm, 0, keepdims=True)
-        sum_ref[it, 0] = jnp.concatenate(
-            [jnp.broadcast_to(norm, (4, 128)), jnp.broadcast_to(bent, (4, 128))], 0
-        )
-        reduce_send(it, 0)
-
-        acc_ref[...] = jnp.zeros_like(acc_ref)
-
-        def scatter_step(step, _):
-            bands, places, values = [], [], [[], [], []]
-            for i in range(STEP_K):
-                k = step * STEP_K + i
-                bands.append(band_ref[pl.ds(k, 1), :])
-                places.append(place_ref[pl.ds(k, 1), :])
-                for c in range(3):
-                    values[c].append(t_ref[pl.ds(c * 32 + k, 1), :])
-            acc_ref[...] += spread_dot(
-                jnp.concatenate(bands, 1),
-                jnp.concatenate(places, 1),
-                [jnp.concatenate(v, 1) for v in values],
-            )
+                for s in range(CHUNKS):
+                    u_ref[s, c, k : k + 1, :] = got[c][s : s + 1]
+        gather(0)
+
+        def chunk_step(chunk, _):
+            for r in range(1, len(rounds)):
+
+                @pl.when((it > 0) & (chunk == marks[r]))
+                def _():
+                    reduce_step(it - 1, r)
+
+            element(chunk)
+            gather(chunk + 1)
+            scatter(chunk)
             return 0
 
-        steps = 27 // STEP_K
-        marks = [steps * i // len(rounds) for i in range(len(rounds) + 1)]
-        for r in range(len(rounds)):
-            if r > 0:
-                sum_ref[it, r] = reduce_wait(it, r - 1)
-                reduce_send(it, r)
-            lax.fori_loop(marks[r], marks[r + 1], scatter_step, 0)
+        lax.fori_loop(0, CHUNKS - 1, chunk_step, 0)
+        element(CHUNKS - 1)
+        scatter(CHUNKS - 1)
 
         hanging = [extra_part(acc_ref, c)[4:5] for c in range(3)]
         fold = spread_dot(
@@ -347,12 +393,15 @@
                 send_ref[number, side, c, 0:4, :] = outgoing[c][side * 4 : side * 4 + 4]
                 send_ref[number, side, c, 4:8, :] = copied[c][:, side * 128 : side * 128 + 128]
         copies = exchange(number)
-        total = reduce_wait(it, len(rounds) - 1)
-        norm = jnp.sum(total[0:1], 1, keepdims=True)
-        bent = jnp.sum(total[4:5], 1, keepdims=True)
-        step = norm / bent
+
+        @pl.when(it > 0)
+        def _():
+            reduce_end(it - 1)
+
         for copy in copies:
             copy.wait()
+        step = step_ref[0, 0:1, :]
+        turn = step_ref[1, 0:1, :]
         back = []
         for c in range(3):
             rows = [
@@ -362,21 +411,49 @@
             ]
             back.append(jnp.concatenate(rows, 1))
         returned = spread_dot(shared_band, shared_place, back, extra=False)
+        norm = jnp.zeros((OWN_ROWS, 128), F32)
+        bent = jnp.zeros((OWN_ROWS, 128), F32)
         for c in range(3):
             add = own_part(returned, c)
-            search = ext_ref[c, 0:OWN_ROWS, :]
-            image = part_ref[c] + jnp.concatenate([add[:, 0:128], add[:, 128:256]], 0)
-            sol_ref[c] = sol_ref[c] + step * search
-            residual = res_ref[c] - step * image
+            fresh = part_ref[c] + jnp.concatenate([add[:, 0:128], add[:, 128:256]], 0)
+            sol_ref[c] = sol_ref[c] + step * search_ref[c]
+            residual = res_ref[c] - step * image_ref[c]
             res_ref[c] = residual
-            if it + 1 < ITERS:
-                ext_ref[c, 0:OWN_ROWS, :] = pre_ref[...] * residual
-                for side in range(2):
-                    own = slice(side * 4, side * 4 + 4)
-                    image = recv_ref[number, side, c, 0:4, :] + send_ref[number, side, c, 4:8, :]
-                    gres_ref[c, own, :] = gres_ref[c, own, :] - step * image
-                ext_ref[c, OWN_ROWS : OWN_ROWS + 8, :] = gpre_ref[...] * gres_ref[c]
-
+            search = pre_ref[...] * residual
+            search_ref[c] = search
+            image = image_ref[c] - turn * fresh
+            image_ref[c] = image
+            ext_ref[c, 0:OWN_ROWS, :] = pre_ref[...] * image
+            norm = norm + residual * search
+            bent = bent + search * image
+            ghost = jnp.concatenate(
+                [
+                    recv_ref[number, side, c, 0:4, :] + send_ref[number, side, c, 4:8, :]
+                    for side in range(2)
+                ],
+                0,
+            )
+            ghost = gimage_ref[c] - turn * ghost
+            gimage_ref[c] = ghost
+            ext_ref[c, OWN_ROWS : OWN_ROWS + 8, :] = gpre_ref[...] * ghost
+        sum_ref[it, 0] = jnp.concatenate(
+            [
+                jnp.broadcast_to(jnp.sum(norm, 0, keepdims=True), (4, 128)),
+                jnp.broadcast_to(jnp.sum(bent, 0, keepdims=True), (4, 128)),
+            ],
+            0,
+        )
+        reduce_send(it, 0)
+        return 0
+
+    lax.fori_loop(0, ITERS, iteration, 0)
+    for r in range(1, len(rounds)):
+        reduce_step(ITERS - 1, r)
+    reduce_end(ITERS - 1)
+    step = step_ref[0, 0:1, :]
+    for c in range(3):
+        sol_ref[c] = sol_ref[c] + step * search_ref[c]
+        res_ref[c] = res_ref[c] - step * image_ref[c]
     for it in range(ITERS):
         for r, (_, _, size) in enumerate(rounds):
             block = red_ref.at[it, r, pl.ds(0, size - 1)]
@@ -407,14 +484,19 @@
             out_specs=(vmem, vmem),
             scratch_shapes=[
                 pltpu.VMEM((3, 80, 128), F32),
+                pltpu.VMEM((3, OWN_ROWS, 128), F32),
+                pltpu.VMEM((3, OWN_ROWS, 128), F32),
                 pltpu.VMEM((3, 8, 128), F32),
                 pltpu.VMEM((8, 128), F32),
+                pltpu.VMEM((1, 1024), F32),
+                pltpu.VMEM((2, 96, 96), BF16),
                 pltpu.VMEM((32, 1024), jnp.int32),
                 pltpu.VMEM((32, 1024), jnp.int32),
-                pltpu.VMEM((3, 32, 1024), F32),
-                pltpu.VMEM((96, 1024), F32),
+                pltpu.VMEM((CHUNKS, 3, 32, 128), F32),
+                pltpu.VMEM((2, 96, 128), F32),
                 pltpu.VMEM((240, 256), F32),
                 pltpu.VMEM((3, OWN_ROWS, 128), F32),
+                pltpu.VMEM((2, 8, 128), F32),
                 pltpu.VMEM((ITERS + 1, 2, 3, 8, 128), F32),
                 pltpu.VMEM((ITERS + 1, 2, 3, 8, 128), F32),
                 pltpu.VMEM((ITERS, len(rounds), widest, 8, 128), F32),

time: 78 us -> 73.9 us (0.947)
  Pallas kernels: 74.7 us -> 70.5 us
    pallas_call x1, Pallas kernels: 74.7 us -> 70.5 us  [local(): call(right_side.reshape(3, OWN_ROWS, 128), precond.reshape(OWN_ROWS, 128)...]
where the time goes in v2:
time: 73.9 us; the launch traced here: 73.7 us
  Pallas kernels  70.5 us (95%)
  local copies, waits for them, and re-layouts  1.81 us (2%)
  between operations  1.41 us (2%)
    pallas_call x1, Pallas kernels, local(): call(right_side.reshape(3, OWN_ROWS, 128), precond.reshape(OWN_ROWS, 128)...  70.5 us

profile of v2, /device:TPU:1, one launch (start us, length us, event | category | flops | bytes accessed | tf_op | source)
XLA Modules:
  0.0 73.7 jit_solution(2685636231480918226)
XLA Ops:
  0.6 0.0 copy-start
  1.3 0.0 copy-start.1
  1.3 0.0 copy-start.2
  1.3 0.0 copy-start.3
  1.4 0.0 copy-start.4
  1.4 0.0 copy-start.5
  1.4 0.9 %copy.16 = f32[1,3,64,128]{3,2,1,0:T(8,128)S(1)} copy(f32[1,3,64,128]{3,1,2,0:T(4,128)} %bitcast.17) | data formatting | bytes 196608
  2.3 0.0 copy-done
  2.3 0.0 copy-done.1
  2.3 0.0 copy-done.2
  2.3 0.0 copy-done.3
  2.4 0.0 copy-done.4
  2.4 0.0 copy-done.5
  2.4 70.5 %descent.1 = (f32[3,64,128]{2,1,0:T(8,128)S(1)}, f32[3,64,128]{2,1,0:T(8,128)S(1)}) custom-call(f32[3,64,128]{2,1,0:T(8,128)S(1)} %bitcast.12, f32[64,128]{1,0:T(8,128)S(1)} %bitcast.15, f32[1,1024]{1,0:T(1,128)S(1)} %bitcast.16, f32[81,81]{1,0:T(8,128)S(1)} %copy-done.1, s32[27,1024]{1,0:T(8,128)S(1)} %copy-done, s32[1]{0:T(128)S(6)} %copy.17.live_ref, ...), custom_call_target="tpu_custom_call" | custom-call | tf_op jit(solution)/shard_map/descent/pallas_call | solution.py:514
  72.9 0.8 %copy_bitcast_fusion = (f32[3,8192]{1,0:T(4,128)}, f32[3,8192]{1,0:T(4,128)}) fusion(f32[1,3,64,128]{3,2,1,0:T(8,128)S(1)} %bitcast.14, f32[1,3,64,128]{3,2,1,0:T(8,128)S(1)} %bitcast.13), kind=kLoop, calls=%fused_computation | loop fusion | bytes 393216 | tf_op jit(solution)/shard_map/reshape | solution.py:524
Async XLA Ops:
  0.6 1.7 %copy-start = (s32[27,1024]{1,0:T(8,128)S(1)}, s32[27,1024]{1,0:T(8,128)}, u32[]{:S(2)}) copy-start(s32[27,1024]{1,0:T(8,128)} %cells_ref.1) | copy-start | bytes 331780
  1.3 1.0 %copy-start.1 = (f32[81,81]{1,0:T(8,128)S(1)}, f32[81,81]{1,0:T(8,128)}, u32[]{:S(2)}) copy-start(f32[81,81]{1,0:T(8,128)} %stiff_ref.1) | copy-start | bytes 78736
  1.3 1.0 %copy-start.2 = (f32[8192]{0:T(1024)S(1)}, f32[8192]{0:T(1024)}, u32[]{:S(2)}) copy-start(f32[8192]{0:T(1024)} %param.9) | copy-start | bytes 98308
  1.3 1.0 %copy-start.3 = (f32[1024]{0:T(1024)S(1)}, f32[1024]{0:T(1024)}, u32[]{:S(2)}) copy-start(f32[1024]{0:T(1024)} %param.10) | copy-start | bytes 12292
  1.4 1.0 %copy-start.4 = (s32[2,512]{1,0:T(2,128)S(1)}, s32[2,512]{1,0:T(2,128)}, u32[]{:S(2)}) copy-start(s32[2,512]{1,0:T(2,128)} %shared_ref.1) | copy-start | bytes 12292
  1.4 1.0 %copy-start.5 = (s32[3,256]{1,0:T(4,128)S(1)}, s32[3,256]{1,0:T(4,128)}, u32[]{:S(2)}) copy-start(s32[3,256]{1,0:T(4,128)} %parents_ref.1) | copy-start | bytes 9220

commit v3 on v2

--- a/solution.py
+++ b/solution.py
@@ -136,6 +136,7 @@
     search_ref,
     image_ref,
     gimage_ref,
+    gres_ref,
     gpre_ref,
     weight_ref,
     matrix_ref,
@@ -267,9 +268,9 @@
         own = slice(side * 4, side * 4 + 4)
         gpre_ref[own, :] = recv_ref[0, side, 0, 4:8, :] * has[side]
         for c in range(3):
-            ext_ref[c, OWN_ROWS + side * 4 : OWN_ROWS + side * 4 + 4, :] = (
-                gpre_ref[own, :] * recv_ref[0, side, c, 0:4, :]
-            )
+            ghost = recv_ref[0, side, c, 0:4, :]
+            gres_ref[c, own, :] = ghost
+            ext_ref[c, OWN_ROWS + side * 4 : OWN_ROWS + side * 4 + 4, :] = gpre_ref[own, :] * ghost
 
     def reduce_send(it, r):
         _, _, size = rounds[r]
@@ -307,7 +308,7 @@
         step_ref[1] = step
 
     fields = [lambda row, c=c: ext_ref[c, row : row + 1, :] for c in range(3)]
-    marks = [1 + (6 * r) // len(rounds) for r in range(len(rounds))]
+    marks = [2 * r - 1 for r in range(len(rounds))]
 
     def columns_of(chunk):
         if isinstance(chunk, int):
@@ -398,10 +399,37 @@
         def _():
             reduce_end(it - 1)
 
+        step = step_ref[0, 0:1, :]
+        turn = step_ref[1, 0:1, :]
+        norm = jnp.zeros((OWN_ROWS, 128), F32)
+        bent = jnp.zeros((OWN_ROWS, 128), F32)
+        bent_copies = jnp.zeros((8, 128), F32)
+        for c in range(3):
+            sol_ref[c] = sol_ref[c] + step * search_ref[c]
+            residual = res_ref[c] - step * image_ref[c]
+            res_ref[c] = residual
+            search = pre_ref[...] * residual
+            search_ref[c] = search
+            image = image_ref[c] - turn * part_ref[c]
+            image_ref[c] = image
+            norm = norm + residual * search
+            bent = bent + search * image
+            ghost = gres_ref[c] - step * gimage_ref[c]
+            gres_ref[c] = ghost
+            mine = jnp.concatenate([send_ref[number, side, c, 4:8, :] for side in range(2)], 0)
+            bent_copies = bent_copies + gpre_ref[...] * ghost * mine
+        bent = jnp.sum(bent, 0, keepdims=True) - turn * jnp.sum(bent_copies, 0, keepdims=True)
+        sum_ref[it, 0] = jnp.concatenate(
+            [
+                jnp.broadcast_to(jnp.sum(norm, 0, keepdims=True), (4, 128)),
+                jnp.broadcast_to(bent, (4, 128)),
+            ],
+            0,
+        )
+        reduce_send(it, 0)
+
         for copy in copies:
             copy.wait()
-        step = step_ref[0, 0:1, :]
-        turn = step_ref[1, 0:1, :]
         back = []
         for c in range(3):
             rows = [
@@ -411,21 +439,11 @@
             ]
             back.append(jnp.concatenate(rows, 1))
         returned = spread_dot(shared_band, shared_place, back, extra=False)
-        norm = jnp.zeros((OWN_ROWS, 128), F32)
-        bent = jnp.zeros((OWN_ROWS, 128), F32)
         for c in range(3):
             add = own_part(returned, c)
-            fresh = part_ref[c] + jnp.concatenate([add[:, 0:128], add[:, 128:256]], 0)
-            sol_ref[c] = sol_ref[c] + step * search_ref[c]
-            residual = res_ref[c] - step * image_ref[c]
-            res_ref[c] = residual
-            search = pre_ref[...] * residual
-            search_ref[c] = search
-            image = image_ref[c] - turn * fresh
+            image = image_ref[c] - turn * jnp.concatenate([add[:, 0:128], add[:, 128:256]], 0)
             image_ref[c] = image
             ext_ref[c, 0:OWN_ROWS, :] = pre_ref[...] * image
-            norm = norm + residual * search
-            bent = bent + search * image
             ghost = jnp.concatenate(
                 [
                     recv_ref[number, side, c, 0:4, :] + send_ref[number, side, c, 4:8, :]
@@ -436,14 +454,6 @@
             ghost = gimage_ref[c] - turn * ghost
             gimage_ref[c] = ghost
             ext_ref[c, OWN_ROWS : OWN_ROWS + 8, :] = gpre_ref[...] * ghost
-        sum_ref[it, 0] = jnp.concatenate(
-            [
-                jnp.broadcast_to(jnp.sum(norm, 0, keepdims=True), (4, 128)),
-                jnp.broadcast_to(jnp.sum(bent, 0, keepdims=True), (4, 128)),
-            ],
-            0,
-        )
-        reduce_send(it, 0)
         return 0
 
     lax.fori_loop(0, ITERS, iteration, 0)
@@ -464,7 +474,7 @@
     rounds = []
     rest, stride = n_cur, 1
     while rest > 1:
-        size = min(8, rest)
+        size = min(32, rest)
         rounds.append(("cur", stride, size))
         stride, rest = stride * size, rest // size
     if n_grp > 1:
@@ -486,6 +496,7 @@
                 pltpu.VMEM((3, 80, 128), F32),
                 pltpu.VMEM((3, OWN_ROWS, 128), F32),
                 pltpu.VMEM((3, OWN_ROWS, 128), F32),
+                pltpu.VMEM((3, 8, 128), F32),
                 pltpu.VMEM((3, 8, 128), F32),
                 pltpu.VMEM((8, 128), F32),
                 pltpu.VMEM((1, 1024), F32),

time: 73.9 us -> 67.4 us (0.912)
  Pallas kernels: 70.5 us -> 63.5 us
    pallas_call x1, Pallas kernels: 70.5 us -> 63.5 us  [local(): call(right_side.reshape(3, OWN_ROWS, 128), precond.reshape(OWN_ROWS, 128)...]
where the time goes in v3:
time: 67.4 us; the launch traced here: 66.8 us
  Pallas kernels  63.5 us (94%)
  local copies, waits for them, and re-layouts  1.81 us (3%)
  between operations  1.41 us (2%)
    pallas_call x1, Pallas kernels, local(): call(right_side.reshape(3, OWN_ROWS, 128), precond.reshape(OWN_ROWS, 128)...  63.5 us

profile of v3, /device:TPU:1, one launch (start us, length us, event | category | flops | bytes accessed | tf_op | source)
XLA Modules:
  0.0 66.8 jit_solution(13204247801880092021)
XLA Ops:
  0.6 0.0 copy-start
  1.3 0.0 copy-start.1
  1.3 0.0 copy-start.2
  1.3 0.0 copy-start.3
  1.4 0.0 copy-start.4
  1.4 0.0 copy-start.5
  1.4 0.9 %copy.16 = f32[1,3,64,128]{3,2,1,0:T(8,128)S(1)} copy(f32[1,3,64,128]{3,1,2,0:T(4,128)} %bitcast.17) | data formatting | bytes 196608
  2.3 0.0 copy-done
  2.3 0.0 copy-done.1
  2.3 0.0 copy-done.2
  2.3 0.0 copy-done.3
  2.4 0.0 copy-done.4
  2.4 0.0 copy-done.5
  2.4 63.5 %descent.1 = (f32[3,64,128]{2,1,0:T(8,128)S(1)}, f32[3,64,128]{2,1,0:T(8,128)S(1)}) custom-call(f32[3,64,128]{2,1,0:T(8,128)S(1)} %bitcast.12, f32[64,128]{1,0:T(8,128)S(1)} %bitcast.15, f32[1,1024]{1,0:T(1,128)S(1)} %bitcast.16, f32[81,81]{1,0:T(8,128)S(1)} %copy-done.1, s32[27,1024]{1,0:T(8,128)S(1)} %copy-done, s32[1]{0:T(128)S(6)} %copy.17.live_ref, ...), custom_call_target="tpu_custom_call" | custom-call | tf_op jit(solution)/shard_map/descent/pallas_call | solution.py:525
  65.9 0.8 %copy_bitcast_fusion = (f32[3,8192]{1,0:T(4,128)}, f32[3,8192]{1,0:T(4,128)}) fusion(f32[1,3,64,128]{3,2,1,0:T(8,128)S(1)} %bitcast.14, f32[1,3,64,128]{3,2,1,0:T(8,128)S(1)} %bitcast.13), kind=kLoop, calls=%fused_computation | loop fusion | bytes 393216 | tf_op jit(solution)/shard_map/reshape | solution.py:535
Async XLA Ops:
  0.6 1.7 %copy-start = (s32[27,1024]{1,0:T(8,128)S(1)}, s32[27,1024]{1,0:T(8,128)}, u32[]{:S(2)}) copy-start(s32[27,1024]{1,0:T(8,128)} %cells_ref.1) | copy-start | bytes 331780
  1.3 1.0 %copy-start.1 = (f32[81,81]{1,0:T(8,128)S(1)}, f32[81,81]{1,0:T(8,128)}, u32[]{:S(2)}) copy-start(f32[81,81]{1,0:T(8,128)} %stiff_ref.1) | copy-start | bytes 78736
  1.3 1.0 %copy-start.2 = (f32[8192]{0:T(1024)S(1)}, f32[8192]{0:T(1024)}, u32[]{:S(2)}) copy-start(f32[8192]{0:T(1024)} %param.9) | copy-start | bytes 98308
  1.3 1.0 %copy-start.3 = (f32[1024]{0:T(1024)S(1)}, f32[1024]{0:T(1024)}, u32[]{:S(2)}) copy-start(f32[1024]{0:T(1024)} %param.10) | copy-start | bytes 12292
  1.4 1.0 %copy-start.4 = (s32[2,512]{1,0:T(2,128)S(1)}, s32[2,512]{1,0:T(2,128)}, u32[]{:S(2)}) copy-start(s32[2,512]{1,0:T(2,128)} %shared_ref.1) | copy-start | bytes 12292
  1.4 1.0 %copy-start.5 = (s32[3,256]{1,0:T(4,128)S(1)}, s32[3,256]{1,0:T(4,128)}, u32[]{:S(2)}) copy-start(s32[3,256]{1,0:T(4,128)} %parents_ref.1) | copy-start | bytes 9220

commit v4 on v2

v4 whole, which is shorter than its diff:
```python
import functools

import jax
import jax.numpy as jnp
from jax import lax
from jax.experimental import pallas as pl
from jax.experimental.pallas import tpu as pltpu
from jax.sharding import PartitionSpec as P

ITERS = 3
F32 = jnp.float32
BF16 = jnp.bfloat16
MESH = pl.DeviceIdType.MESH
OWN_ROWS = 64
NEAR = slice(64, 80)
GHOSTS = slice(64, 72)
SHARED = slice(72, 80)
EXT_ROWS = 82
EARLY = 3
CHUNKS = 8
NODES = 28


def take(src, lanes):
    return jnp.take_along_axis(src, lanes, axis=1, mode="promise_in_bounds")


def gather_tile(fields, rows, index, found=None):
    lanes = index & 127
    own = index >> 7
    found = list(found) if found else [jnp.zeros((8, 128), F32) for _ in fields]
    for row in rows:
        hit = own == row
        for i, field in enumerate(fields):
            line = jnp.broadcast_to(field(row), (8, 128))
            found[i] = jnp.where(hit, take(line, lanes), found[i])
    return found


def folded(index):
    row = index >> 7
    lane = index & 127
    own = row < 64
    hang = row >= 80
    near = 32 + (row & 3) + jnp.where(row >= 72, 4, 0)
    band = jnp.where(own, row & 31, jnp.where(hang, 40, near))
    half = jnp.where(own, row >> 5, jnp.where(hang, row & 1, (row >> 2) & 1))
    return band, half * 128 + lane


def pieces(row):
    high = row.astype(BF16)
    low = (row - high.astype(F32)).astype(BF16)
    return high, low


def spread_dot(band, place, values, extra=True):
    n = band.shape[1]
    band16 = band.astype(jnp.int16)
    place16 = place.astype(jnp.int16)
    zero = jnp.zeros((16, n), BF16)
    one = jnp.ones((256, n), BF16)
    hot = jnp.where(
        lax.broadcasted_iota(jnp.int16, (256, n), 0) == place16, one, jnp.zeros((256, n), BF16)
    )
    line = lax.broadcasted_iota(jnp.int16, (16, n), 0)
    hit0 = line == band16
    hit1 = (line + jnp.int16(16)) == band16
    parts = []
    tails = []
    if extra:
        first = line < jnp.int16(8)
        hit2 = jnp.where(first, line, line - jnp.int16(8)) == (band16 - jnp.int16(32))
    for value in values:
        high, low = pieces(value)
        high = jnp.broadcast_to(high, (16, n))
        low = jnp.broadcast_to(low, (16, n))
        for piece in (high, low):
            parts.append(jnp.where(hit0, piece, zero))
            parts.append(jnp.where(hit1, piece, zero))
        if extra:
            tails.append(jnp.where(hit2, jnp.where(first, high, low), zero))
    left = jnp.concatenate(parts + tails, 0)
    return lax.dot_general(left, hot, (((1,), (1,)), ((), ())), preferred_element_type=F32)


def own_part(total, c):
    return total[c * 64 : c * 64 + 32] + total[c * 64 + 32 : c * 64 + 64]


def extra_part(total, c):
    return total[192 + c * 16 : 200 + c * 16] + total[200 + c * 16 : 208 + c * 16]


def hang_part(total, c):
    return total[240 + 2 * c : 241 + 2 * c] + total[241 + 2 * c : 242 + 2 * c]


def as_row(block):
    return jnp.concatenate([block[i : i + 1] for i in range(block.shape[0])], 1)


def halves(wide):
    return jnp.concatenate([wide[:, 0:128], wide[:, 128:256]], 0)


def near_rows(wide):
    return jnp.concatenate(
        [wide[0:4, 0:128], wide[0:4, 128:256], wide[4:8, 0:128], wide[4:8, 128:256]], 0
    )


def chunk_dot(band_ref, place_ref, piece_ref, columns):
    zero = jnp.zeros((16, 128), BF16)
    one = jnp.ones((16, 128), BF16)
    line = lax.broadcasted_iota(jnp.int16, (16, 128), 0)
    lines = [line + jnp.int16(16 * i) for i in range(16)]
    first = line < jnp.int16(8)
    beyond = jnp.where(first, line, line - jnp.int16(8)) + jnp.int16(32)
    hots, lefts = [], []
    for k in range(NODES):
        band = jnp.broadcast_to(band_ref[k : k + 1, columns], (16, 128)).astype(jnp.int16)
        place = jnp.broadcast_to(place_ref[k : k + 1, columns], (16, 128)).astype(jnp.int16)
        hots.append(jnp.concatenate([jnp.where(at == place, one, zero) for at in lines], 0))
        hits = [lines[0] == band, lines[1] == band]
        hit_beyond = beyond == band
        parts, tails = [], []
        for c in range(3):
            row = k * 8 + c * 2
            pair = [
                jnp.broadcast_to(piece_ref[row + p : row + p + 1, :], (16, 128)).astype(BF16)
                for p in range(2)
            ]
            parts += [jnp.where(hit, piece, zero) for piece in pair for hit in hits]
            tails.append(jnp.where(hit_beyond, jnp.where(first, pair[0], pair[1]), zero))
        block = piece_ref[k * 8 : k * 8 + 8, :]
        block = jnp.concatenate([block, jnp.zeros((8, 128), F32)], 0).astype(BF16)
        tails.append(jnp.where(band == jnp.int16(40), block, zero))
        lefts.append(jnp.concatenate(parts + tails, 0))
    return lax.dot_general(
        jnp.concatenate(lefts, 1),
        jnp.concatenate(hots, 1),
        (((1,), (1,)), ((), ())),
        preferred_element_type=F32,
    )


def kernel(
    rounds,
    sizes,
    rhs_ref,
    prec_ref,
    visc_ref,
    stiff_ref,
    cells_ref,
    live_ref,
    shared_ref,
    parents_ref,
    sol_ref,
    res_ref,
    ext_ref,
    x_ref,
    r_ref,
    search_ref,
    image_ref,
    pre_ref,
    where_ref,
    weight_ref,
    matrix_ref,
    node_ref,
    tail_ref,
    band_ref,
    place_ref,
    u_ref,
    tail_u_ref,
    hang_ref,
    piece_ref,
    acc_ref,
    step_ref,
    send_ref,
    recv_ref,
    red_ref,
    sum_ref,
    send_sem,
    recv_sem,
    rsend_sem,
    rrecv_sem,
):
    n_grp, n_cur = sizes
    devices = n_grp * n_cur
    my_grp = lax.axis_index("grp")
    my_cur = lax.axis_index("cur")
    me = my_grp * n_cur + my_cur

    def ring(offset):
        other = lax.rem(me + offset + devices, devices)
        return {"grp": other // n_cur, "cur": lax.rem(other, n_cur)}

    def my_place(r):
        axis, stride, size = rounds[r]
        mine = my_cur if axis == "cur" else my_grp
        return lax.rem(mine // stride, size)

    def partner(r, j):
        axis, stride, size = rounds[r]
        mine = my_cur if axis == "cur" else my_grp
        place = my_place(r)
        return {axis: mine + (lax.rem(place + j, size) - place) * stride}

    barrier = pltpu.get_barrier_semaphore()
    targets = [ring(-1), ring(1)]
    for r, (_, _, size) in enumerate(rounds):
        targets += [partner(r, j) for j in range(1, size)]
    for target in targets:
        pl.semaphore_signal(barrier, inc=1, device_id=target, device_id_type=MESH)

    has = [
        jnp.where(me > 0, 1.0, 0.0).astype(F32),
        jnp.where(me < devices - 1, 1.0, 0.0).astype(F32),
    ]

    def exchange(number):
        copies = []
        for side, offset in ((0, -1), (1, 1)):
            copies.append(
                pltpu.make_async_remote_copy(
                    src_ref=send_ref.at[number, side],
                    dst_ref=recv_ref.at[number, 1 - side],
                    send_sem=send_sem.at[number, side],
                    recv_sem=recv_sem.at[number, 1 - side],
                    device_id=ring(offset),
                    device_id_type=MESH,
                )
            )
        return copies

    def reduce_send(it, r):
        _, _, size = rounds[r]
        spot = my_place(r)
        red_ref[it, r, spot] = sum_ref[it, r]
        for j in range(1, size):
            pltpu.make_async_remote_copy(
                src_ref=sum_ref.at[it, r],
                dst_ref=red_ref.at[it, r, spot],
                send_sem=rsend_sem.at[it, r],
                recv_sem=rrecv_sem.at[it, r],
                device_id=partner(r, j),
                device_id_type=MESH,
            ).start()

    def reduce_wait(it, r):
        _, _, size = rounds[r]
        block = red_ref.at[it, r, pl.ds(0, size - 1)]
        pltpu.make_async_copy(block, block, rrecv_sem.at[it, r]).wait()
        total = red_ref[it, r, 0]
        for j in range(1, size):
            total = total + red_ref[it, r, j]
        return total

    def reduce_step(it, r):
        sum_ref[it, r] = reduce_wait(it, r - 1)
        reduce_send(it, r)

    def reduce_end(it):
        total = reduce_wait(it, len(rounds) - 1)
        norm = jnp.sum(total[0:1], 1, keepdims=True)
        bent = jnp.sum(total[4:5], 1, keepdims=True)
        step = jnp.broadcast_to(norm / bent, (8, 128))
        step_ref[0] = step
        step_ref[1] = step

    shared_index = jnp.concatenate(
        [shared_ref[j : j + 1, q * 128 : (q + 1) * 128] for j in range(2) for q in range(4)], 0
    )
    outgoing = gather_tile(
        [lambda row, c=c: rhs_ref[c, row : row + 1, :] for c in range(3)]
        + [lambda row: prec_ref[row : row + 1, :]],
        range(OWN_ROWS),
        shared_index,
    )
    for side in range(2):
        for c in range(3):
            send_ref[0, side, c, 0:4, :] = outgoing[c][side * 4 : side * 4 + 4]
            send_ref[0, side, c, 4:8, :] = outgoing[3][side * 4 : side * 4 + 4]
    pl.semaphore_wait(barrier, len(targets))
    for copy in exchange(0):
        copy.start()

    shared_band, shared_place = folded(
        jnp.concatenate([shared_ref[0:1, :], shared_ref[1:2, :]], 1)
    )
    count = (lax.broadcasted_iota(jnp.int32, (1, 1024), 1) + 1).astype(F32)
    where_ref[...] = halves(own_part(spread_dot(shared_band, shared_place, [count], False), 0))

    def moved(index):
        found = gather_tile([lambda row: where_ref[row : row + 1, :]], range(OWN_ROWS), index)[0]
        beyond = jnp.where(index >= 72 * 128, index + 1024, index)
        return jnp.where(found > 0.5, found.astype(jnp.int32) + (72 * 128 - 1), beyond)

    stays = where_ref[...] < 0.5
    pre_ref[0:OWN_ROWS, :] = jnp.where(stays, prec_ref[...], 0.0)
    pre_ref[SHARED, :] = outgoing[3]
    pre_ref[GHOSTS, :] = jnp.zeros((8, 128), F32)
    for c in range(3):
        r_ref[c, 0:OWN_ROWS, :] = jnp.where(stays, rhs_ref[c], 0.0)
        r_ref[c, SHARED, :] = outgoing[c]
        r_ref[c, GHOSTS, :] = jnp.zeros((8, 128), F32)
        search = pre_ref[...] * r_ref[c]
        search_ref[c] = search
        ext_ref[c, 0:80, :] = search
    x_ref[...] = jnp.zeros_like(x_ref)
    image_ref[...] = jnp.zeros_like(image_ref)
    u_ref[...] = jnp.zeros_like(u_ref)
    piece_ref[...] = jnp.zeros_like(piece_ref)
    step_ref[0] = jnp.zeros((8, 128), F32)
    step_ref[1] = jnp.full((8, 128), -1.0, F32)

    band_ref[24:32, :] = jnp.zeros((8, 1024), jnp.int32)
    place_ref[24:32, :] = jnp.zeros((8, 1024), jnp.int32)
    parent_rows = [parents_ref[p : p + 1, q * 128 : (q + 1) * 128] for p in range(3) for q in range(2)]
    parent_index = moved(jnp.concatenate(parent_rows + parent_rows[:2], 0))
    parent_band, parent_place = folded(as_row(parent_index[0:6]))
    for k in range(24, 27):
        index = moved(
            jnp.concatenate([cells_ref[k : k + 1, s * 128 : s * 128 + 128] for s in range(8)], 0)
        )
        tail_ref[k - 24] = index
        band, place = folded(index)
        band_ref[k : k + 1, :] = as_row(band)
        place_ref[k : k + 1, :] = as_row(place)

    def columns_of(chunk):
        if isinstance(chunk, int):
            return pl.ds(chunk * 128, 128)
        return pl.ds(pl.multiple_of(chunk * 128, 128), 128)

    def move_chunk(chunk, _):
        for top in range(0, 24, 8):
            index = moved(cells_ref[top : top + 8, columns_of(chunk)])
            node_ref[top : top + 8, columns_of(chunk)] = index
            band, place = folded(index)
            band_ref[top : top + 8, columns_of(chunk)] = band
            place_ref[top : top + 8, columns_of(chunk)] = place
        return 0

    lax.fori_loop(0, CHUNKS, move_chunk, 0)
    slot = lax.broadcasted_iota(jnp.int32, (1, 1024), 1)
    weight_ref[...] = jnp.where(slot < live_ref[0], visc_ref[...], 0.0)
    at = lax.broadcasted_iota(jnp.int32, (96, 81), 0)
    want = jnp.where((at & 31) < 27, (at >> 5) * 27 + (at & 31), -1)
    pick = jnp.where(want == lax.broadcasted_iota(jnp.int32, (96, 81), 1), 1.0, 0.0).astype(BF16)

    def padded(part):
        rows = lax.dot_general(pick, part, (((1,), (1,)), ((), ())), preferred_element_type=F32)
        return lax.dot_general(
            rows.astype(BF16), pick, (((1,), (1,)), ((), ())), preferred_element_type=F32
        ).astype(BF16)

    stiff = stiff_ref[...]
    stiff_high = stiff.astype(BF16)
    matrix_ref[0] = padded(stiff_high)
    matrix_ref[1] = padded((stiff - stiff_high.astype(F32)).astype(BF16))

    fields = [lambda row, c=c: ext_ref[c, row : row + 1, :] for c in range(3)]
    early = range(OWN_ROWS)
    late = range(OWN_ROWS, EXT_ROWS)

    def gather(chunk, rows, go_on):
        for top in range(0, 24, 8):
            start = [u_ref[chunk, c, top : top + 8, :] for c in range(3)] if go_on else None
            got = gather_tile(fields, rows, node_ref[top : top + 8, columns_of(chunk)], start)
            for c in range(3):
                u_ref[chunk, c, top : top + 8, :] = got[c]

    def element(chunk):
        u = u_ref[chunk].reshape(96, 128)
        u_high = u.astype(BF16)
        u_low = (u - u_high.astype(F32)).astype(BF16)
        high, low = matrix_ref[0], matrix_ref[1]
        t = (
            jnp.dot(high, u_high, preferred_element_type=F32)
            + jnp.dot(high, u_low, preferred_element_type=F32)
            + jnp.dot(low, u_high, preferred_element_type=F32)
        ) * weight_ref[0:1, columns_of(chunk)]
        t_high = t.astype(BF16).astype(F32)
        t_low = t - t_high
        for c in range(3):
            own = slice(c * 32, c * 32 + 32)
            piece_ref[pl.ds(2 * c, 32, stride=8), :] = t_high[own]
            piece_ref[pl.ds(2 * c + 1, 32, stride=8), :] = t_low[own]

    def scatter(chunk):
        acc_ref[...] += chunk_dot(band_ref, place_ref, piece_ref, columns_of(chunk))

    def near_sums(number, c):
        return jnp.concatenate(
            [recv_ref[number, side, c, 0:4, :] for side in range(2)]
            + [recv_ref[number, side, c, 4:8, :] * has[side] for side in range(2)],
            0,
        )

    def finish_near(number):
        turn = step_ref[1, 0:1, :]
        for c in range(3):
            image = image_ref[c, NEAR, :] - turn * near_sums(number, c)
            image_ref[c, NEAR, :] = image
            ext_ref[c, NEAR, :] = pre_ref[NEAR, :] * image

    def iteration(it, _):
        for c, got in enumerate(gather_tile(fields, early, parent_index)):
            hang_ref[c] = got
        for k in range(3):
            for c, got in enumerate(gather_tile(fields, early, tail_ref[k])):
                tail_u_ref[k, c] = got

        def early_step(chunk, _):
            gather(chunk, early, False)
            return 0

        lax.fori_loop(0, EARLY, early_step, 0)

        @pl.when(it > 0)
        def _():
            for r in range(1, len(rounds)):
                reduce_step(it - 1, r)

        for copy in exchange(it):
            copy.wait()

        @pl.when(it == 0)
        def _():
            for side in range(2):
                own = slice(64 + side * 4, 68 + side * 4)
                scale = recv_ref[0, side, 0, 4:8, :] * has[side]
                pre_ref[own, :] = scale
                for c in range(3):
                    ghost = recv_ref[0, side, c, 0:4, :]
                    r_ref[c, own, :] = ghost
                    ext_ref[c, own, :] = scale * ghost

        @pl.when(it > 0)
        def _():
            finish_near(it)

        found = gather_tile(
            fields, range(OWN_ROWS, 80), parent_index, [hang_ref[c] for c in range(3)]
        )
        for c in range(3):
            ext_ref[c, 80:82, :] = (
                0.375 * found[c][0:2] + 0.75 * found[c][2:4] - 0.125 * found[c][4:6]
            )
        acc_ref[...] = jnp.zeros_like(acc_ref)
        for k in range(3):
            got = gather_tile(fields, late, tail_ref[k], [tail_u_ref[k, c] for c in range(3)])
            for c in range(3):
                for s in range(CHUNKS):
                    u_ref[s, c, 24 + k : 25 + k, :] = got[c][s : s + 1]
        gather(0, late, True)

        def late_step(chunk, _):
            element(chunk)
            gather(chunk + 1, late, True)
            scatter(chunk)
            return 0

        def whole_step(chunk, _):
            element(chunk)
            gather(chunk + 1, range(EXT_ROWS), False)
            scatter(chunk)
            return 0

        lax.fori_loop(0, EARLY - 1, late_step, 0)
        if EARLY < CHUNKS:
            lax.fori_loop(EARLY - 1, CHUNKS - 1, whole_step, 0)
        element(CHUNKS - 1)
        scatter(CHUNKS - 1)

        hanging = [hang_part(acc_ref, c) for c in range(3)]
        fold = spread_dot(
            parent_band,
            parent_place,
            [jnp.concatenate([0.375 * h, 0.75 * h, -0.125 * h], 1) for h in hanging],
        )
        number = it + 1
        near = []
        for c in range(3):
            near.append(near_rows(extra_part(acc_ref, c) + extra_part(fold, c)))
            for side in range(2):
                send_ref[number, side, c, 0:4, :] = near[c][8 + side * 4 : 12 + side * 4]
                send_ref[number, side, c, 4:8, :] = near[c][side * 4 : side * 4 + 4]
        for copy in exchange(number):
            copy.start()

        @pl.when(it > 0)
        def _():
            reduce_end(it - 1)

        step = step_ref[0, 0:1, :]
        turn = step_ref[1, 0:1, :]
        norm = jnp.zeros((1, 128), F32)
        bent = jnp.zeros((1, 128), F32)
        for c in range(3):
            x_ref[c] = x_ref[c] + step * search_ref[c]
            residual = r_ref[c] - step * image_ref[c]
            r_ref[c] = residual
            search = pre_ref[...] * residual
            search_ref[c] = search
            part = jnp.concatenate([halves(own_part(acc_ref, c) + own_part(fold, c)), near[c]], 0)
            change = turn * part
            image = image_ref[c] - change
            image_ref[c] = image
            ext_ref[c, 0:OWN_ROWS, :] = pre_ref[0:OWN_ROWS, :] * image[0:OWN_ROWS]
            for own in (slice(0, OWN_ROWS), SHARED):
                norm = norm + jnp.sum(residual[own] * search[own], 0, keepdims=True)
                bent = bent + jnp.sum(search[own] * image[own], 0, keepdims=True)
            bent = bent - jnp.sum(search[GHOSTS] * change[GHOSTS], 0, keepdims=True)
        sum_ref[it, 0] = jnp.concatenate(
            [jnp.broadcast_to(norm, (4, 128)), jnp.broadcast_to(bent, (4, 128))], 0
        )
        reduce_send(it, 0)
        return 0

    lax.fori_loop(0, ITERS, iteration, 0)
    for copy in exchange(ITERS):
        copy.wait()
    finish_near(ITERS)
    last = ITERS - 1
    home = []
    for values_ref in (x_ref, search_ref, r_ref, image_ref):
        home.append(
            spread_dot(
                shared_band, shared_place, [as_row(values_ref[c, SHARED, :]) for c in range(3)], False
            )
        )
    for r in range(1, len(rounds)):
        reduce_step(last, r)
    reduce_end(last)
    step = step_ref[0, 0:1, :]

    def whole(values_ref, spread, c):
        return values_ref[c, 0:OWN_ROWS, :] + halves(own_part(spread, c))

    for c in range(3):
        sol_ref[c] = whole(x_ref, home[0], c) + step * whole(search_ref, home[1], c)
        res_ref[c] = whole(r_ref, home[2], c) - step * whole(image_ref, home[3], c)
    for it in range(ITERS):
        for r, (_, _, size) in enumerate(rounds):
            block = red_ref.at[it, r, pl.ds(0, size - 1)]
            pltpu.make_async_copy(block, block, rsend_sem.at[it, r]).wait()


def make_local(n_grp, n_cur):
    rounds = []
    rest, stride = n_cur, 1
    while rest > 1:
        size = min(32, rest)
        rounds.append(("cur", stride, size))
        stride, rest = stride * size, rest // size
    if n_grp > 1:
        rounds.append(("grp", 1, n_grp))
    widest = max(size for _, _, size in rounds)

    def local(
        right_side, precond, viscosity, stiffness, element_nodes, live, shared, parents
    ):
        vmem = pl.BlockSpec(memory_space=pltpu.VMEM)
        smem = pl.BlockSpec(memory_space=pltpu.SMEM)
        shape = jax.ShapeDtypeStruct((3, OWN_ROWS, 128), F32)
        call = pl.pallas_call(
            functools.partial(kernel, tuple(rounds), (n_grp, n_cur)),
            out_shape=(shape, shape),
            in_specs=[vmem, vmem, vmem, vmem, vmem, smem, vmem, vmem],
            out_specs=(vmem, vmem),
            scratch_shapes=[
                pltpu.VMEM((3, 88, 128), F32),
                pltpu.VMEM((3, 80, 128), F32),
                pltpu.VMEM((3, 80, 128), F32),
                pltpu.VMEM((3, 80, 128), F32),
                pltpu.VMEM((3, 80, 128), F32),
                pltpu.VMEM((80, 128), F32),
                pltpu.VMEM((OWN_ROWS, 128), F32),
                pltpu.VMEM((1, 1024), F32),
                pltpu.VMEM((2, 96, 96), BF16),
                pltpu.VMEM((24, 1024), jnp.int32),
                pltpu.VMEM((3, 8, 128), jnp.int32),
                pltpu.VMEM((32, 1024), jnp.int32),
                pltpu.VMEM((32, 1024), jnp.int32),
                pltpu.VMEM((CHUNKS, 3, 32, 128), F32),
                pltpu.VMEM((3, 3, 8, 128), F32),
                pltpu.VMEM((3, 8, 128), F32),
                pltpu.VMEM((256, 128), F32),
                pltpu.VMEM((256, 256), F32),
                pltpu.VMEM((2, 8, 128), F32),
                pltpu.VMEM((ITERS + 1, 2, 3, 8, 128), F32),
                pltpu.VMEM((ITERS + 1, 2, 3, 8, 128), F32),
                pltpu.VMEM((ITERS, len(rounds), widest, 8, 128), F32),
                pltpu.VMEM((ITERS, len(rounds), 8, 128), F32),
                pltpu.SemaphoreType.DMA((ITERS + 1, 2)),
                pltpu.SemaphoreType.DMA((ITERS + 1, 2)),
                pltpu.SemaphoreType.DMA((ITERS, len(rounds))),
                pltpu.SemaphoreType.DMA((ITERS, len(rounds))),
            ],
            compiler_params=pltpu.CompilerParams(
                collective_id=0, has_side_effects=True, vmem_limit_bytes=48 * 1024 * 1024
            ),
            name="descent",
        )
        sol, res = call(
            right_side.reshape(3, OWN_ROWS, 128),
            precond.reshape(OWN_ROWS, 128),
            viscosity.reshape(1, 1024),
            stiffness,
            element_nodes,
            live,
            shared,
            parents,
        )
        return sol.reshape(3, OWN_ROWS * 128), res.reshape(3, OWN_ROWS * 128)

    return local


def solution(mesh):
    both = ("grp", "cur")
    in_specs = (
        P(None, both),
        P(both),
        P(both),
        P(),
        P(None, both),
        P(both),
        P(None, both),
        P(None, both),
    )
    out_specs = (P(None, both), P(None, both))
    return jax.shard_map(
        make_local(mesh.shape["grp"], mesh.shape["cur"]),
        mesh=mesh,
        in_specs=in_specs,
        out_specs=out_specs,
        check_vma=False,
    )
```

time: 73.9 us -> 64.9 us (0.88)
  Pallas kernels: 70.5 us -> 61.6 us
    pallas_call x1, Pallas kernels: 70.5 us -> 61.6 us  [local(): call(right_side.reshape(3, OWN_ROWS, 128), precond.reshape(OWN_ROWS, 128)...]
where the time goes in v4:
time: 64.9 us; the launch traced here: 64.8 us
  Pallas kernels  61.6 us (95%)
  local copies, waits for them, and re-layouts  1.81 us (3%)
  between operations  1.41 us (2%)
    pallas_call x1, Pallas kernels, local(): call(right_side.reshape(3, OWN_ROWS, 128), precond.reshape(OWN_ROWS, 128)...  61.6 us

profile of v4, /device:TPU:1, one launch (start us, length us, event | category | flops | bytes accessed | tf_op | source)
XLA Modules:
  0.0 64.8 jit_solution(12425482719726700132)
XLA Ops:
  0.6 0.0 copy-start
  1.3 0.0 copy-start.1
  1.3 0.0 copy-start.2
  1.3 0.0 copy-start.3
  1.4 0.0 copy-start.4
  1.4 0.0 copy-start.5
  1.4 0.9 %copy.16 = f32[1,3,64,128]{3,2,1,0:T(8,128)S(1)} copy(f32[1,3,64,128]{3,1,2,0:T(4,128)} %bitcast.17) | data formatting | bytes 196608
  2.3 0.0 copy-done
  2.3 0.0 copy-done.1
  2.3 0.0 copy-done.2
  2.3 0.0 copy-done.3
  2.4 0.0 copy-done.4
  2.4 0.0 copy-done.5
  2.4 61.6 %descent.1 = (f32[3,64,128]{2,1,0:T(8,128)S(1)}, f32[3,64,128]{2,1,0:T(8,128)S(1)}) custom-call(f32[3,64,128]{2,1,0:T(8,128)S(1)} %bitcast.12, f32[64,128]{1,0:T(8,128)S(1)} %bitcast.15, f32[1,1024]{1,0:T(1,128)S(1)} %bitcast.16, f32[81,81]{1,0:T(8,128)S(1)} %copy-done.1, s32[27,1024]{1,0:T(8,128)S(1)} %copy-done, s32[1]{0:T(128)S(6)} %copy.17.live_ref, ...), custom_call_target="tpu_custom_call" | custom-call | tf_op jit(solution)/shard_map/descent/pallas_call | solution.py:608
  64.0 0.8 %copy_bitcast_fusion = (f32[3,8192]{1,0:T(4,128)}, f32[3,8192]{1,0:T(4,128)}) fusion(f32[1,3,64,128]{3,2,1,0:T(8,128)S(1)} %bitcast.14, f32[1,3,64,128]{3,2,1,0:T(8,128)S(1)} %bitcast.13), kind=kLoop, calls=%fused_computation | loop fusion | bytes 393216 | tf_op jit(solution)/shard_map/reshape | solution.py:618
Async XLA Ops:
  0.6 1.7 %copy-start = (s32[27,1024]{1,0:T(8,128)S(1)}, s32[27,1024]{1,0:T(8,128)}, u32[]{:S(2)}) copy-start(s32[27,1024]{1,0:T(8,128)} %cells_ref.1) | copy-start | bytes 331780
  1.3 1.0 %copy-start.1 = (f32[81,81]{1,0:T(8,128)S(1)}, f32[81,81]{1,0:T(8,128)}, u32[]{:S(2)}) copy-start(f32[81,81]{1,0:T(8,128)} %stiff_ref.1) | copy-start | bytes 78736
  1.3 1.0 %copy-start.2 = (f32[8192]{0:T(1024)S(1)}, f32[8192]{0:T(1024)}, u32[]{:S(2)}) copy-start(f32[8192]{0:T(1024)} %param.9) | copy-start | bytes 98308
  1.3 1.0 %copy-start.3 = (f32[1024]{0:T(1024)S(1)}, f32[1024]{0:T(1024)}, u32[]{:S(2)}) copy-start(f32[1024]{0:T(1024)} %param.10) | copy-start | bytes 12292
  1.4 1.0 %copy-start.4 = (s32[2,512]{1,0:T(2,128)S(1)}, s32[2,512]{1,0:T(2,128)}, u32[]{:S(2)}) copy-start(s32[2,512]{1,0:T(2,128)} %shared_ref.1) | copy-start | bytes 12292
  1.4 1.0 %copy-start.5 = (s32[3,256]{1,0:T(4,128)S(1)}, s32[3,256]{1,0:T(4,128)}, u32[]{:S(2)}) copy-start(s32[3,256]{1,0:T(4,128)} %parents_ref.1) | copy-start | bytes 9220

commit v5 on v4

--- a/solution.py
+++ b/solution.py
@@ -419,11 +419,6 @@
 
         lax.fori_loop(0, EARLY, early_step, 0)
 
-        @pl.when(it > 0)
-        def _():
-            for r in range(1, len(rounds)):
-                reduce_step(it - 1, r)
-
         for copy in exchange(it):
             copy.wait()
 
@@ -456,6 +451,11 @@
                 for s in range(CHUNKS):
                     u_ref[s, c, 24 + k : 25 + k, :] = got[c][s : s + 1]
         gather(0, late, True)
+
+        @pl.when(it > 0)
+        def _():
+            for r in range(1, len(rounds)):
+                reduce_step(it - 1, r)
 
         def late_step(chunk, _):
             element(chunk)

time: 64.9 us -> 64.2 us (0.989)
  Pallas kernels: 61.6 us -> 60.8 us
    pallas_call x1, Pallas kernels: 61.6 us -> 60.8 us  [local(): call(right_side.reshape(3, OWN_ROWS, 128), precond.reshape(OWN_ROWS, 128)...]
where the time goes in v5:
time: 64.2 us; the launch traced here: 64.1 us
  Pallas kernels  60.8 us (95%)
  local copies, waits for them, and re-layouts  1.81 us (3%)
  between operations  1.41 us (2%)
    pallas_call x1, Pallas kernels, local(): call(right_side.reshape(3, OWN_ROWS, 128), precond.reshape(OWN_ROWS, 128)...  60.8 us

profile of v5, /device:TPU:1, one launch (start us, length us, event | category | flops | bytes accessed | tf_op | source)
XLA Modules:
  0.0 64.1 jit_solution(2258085630706455099)
XLA Ops:
  0.6 0.0 copy-start
  1.3 0.0 copy-start.1
  1.3 0.0 copy-start.2
  1.3 0.0 copy-start.3
  1.4 0.0 copy-start.4
  1.4 0.0 copy-start.5
  1.4 0.9 %copy.16 = f32[1,3,64,128]{3,2,1,0:T(8,128)S(1)} copy(f32[1,3,64,128]{3,1,2,0:T(4,128)} %bitcast.17) | data formatting | bytes 196608
  2.3 0.0 copy-done
  2.3 0.0 copy-done.1
  2.3 0.0 copy-done.2
  2.3 0.0 copy-done.3
  2.4 0.0 copy-done.4
  2.4 0.0 copy-done.5
  2.4 60.8 %descent.1 = (f32[3,64,128]{2,1,0:T(8,128)S(1)}, f32[3,64,128]{2,1,0:T(8,128)S(1)}) custom-call(f32[3,64,128]{2,1,0:T(8,128)S(1)} %bitcast.12, f32[64,128]{1,0:T(8,128)S(1)} %bitcast.15, f32[1,1024]{1,0:T(1,128)S(1)} %bitcast.16, f32[81,81]{1,0:T(8,128)S(1)} %copy-done.1, s32[27,1024]{1,0:T(8,128)S(1)} %copy-done, s32[1]{0:T(128)S(6)} %copy.17.live_ref, ...), custom_call_target="tpu_custom_call" | custom-call | tf_op jit(solution)/shard_map/descent/pallas_call | solution.py:608
  63.2 0.8 %copy_bitcast_fusion = (f32[3,8192]{1,0:T(4,128)}, f32[3,8192]{1,0:T(4,128)}) fusion(f32[1,3,64,128]{3,2,1,0:T(8,128)S(1)} %bitcast.14, f32[1,3,64,128]{3,2,1,0:T(8,128)S(1)} %bitcast.13), kind=kLoop, calls=%fused_computation | loop fusion | bytes 393216 | tf_op jit(solution)/shard_map/reshape | solution.py:618
Async XLA Ops:
  0.6 1.7 %copy-start = (s32[27,1024]{1,0:T(8,128)S(1)}, s32[27,1024]{1,0:T(8,128)}, u32[]{:S(2)}) copy-start(s32[27,1024]{1,0:T(8,128)} %cells_ref.1) | copy-start | bytes 331780
  1.3 1.0 %copy-start.1 = (f32[81,81]{1,0:T(8,128)S(1)}, f32[81,81]{1,0:T(8,128)}, u32[]{:S(2)}) copy-start(f32[81,81]{1,0:T(8,128)} %stiff_ref.1) | copy-start | bytes 78736
  1.3 1.0 %copy-start.2 = (f32[8192]{0:T(1024)S(1)}, f32[8192]{0:T(1024)}, u32[]{:S(2)}) copy-start(f32[8192]{0:T(1024)} %param.9) | copy-start | bytes 98308
  1.3 1.0 %copy-start.3 = (f32[1024]{0:T(1024)S(1)}, f32[1024]{0:T(1024)}, u32[]{:S(2)}) copy-start(f32[1024]{0:T(1024)} %param.10) | copy-start | bytes 12292
  1.4 1.0 %copy-start.4 = (s32[2,512]{1,0:T(2,128)S(1)}, s32[2,512]{1,0:T(2,128)}, u32[]{:S(2)}) copy-start(s32[2,512]{1,0:T(2,128)} %shared_ref.1) | copy-start | bytes 12292
  1.4 1.0 %copy-start.5 = (s32[3,256]{1,0:T(4,128)S(1)}, s32[3,256]{1,0:T(4,128)}, u32[]{:S(2)}) copy-start(s32[3,256]{1,0:T(4,128)} %parents_ref.1) | copy-start | bytes 9220
